TPU v7x, 128 devices: a whole 4x4x4 slice. The times are simulated.
128 devices in a mesh: img: 8 (over x, core), pair: 16 (over y, z).
Axes of the slice: x: 4, y: 4, z: 4, core: 2. Of those that a mesh axis runs over, the one named last changes fastest.
Arguments:
- log_depth: float32 [64, 196608], P('pair', 'img'), may hold values from 0.5 to 1.5
- moment_one: float32 [64, 196608], P('pair', 'img'), may hold values from -6 to 6
- moment_two: float32 [64, 196608], P('pair', 'img'), may hold values from 1 to 16
- image_pose: float32 [7, 64], replicated, may hold values from -1 to 2, as said below
- pair_points: bfloat16 [128, 6, 196608], P('pair', None, 'img'), may hold values from -10 to 24
- confidence: bfloat16 [128, 2, 196608], P('pair', None, 'img'), may hold values from 1 to 8
- pair_pose: float32 [7, 128], P(None, 'pair'), may hold values from -1 to 2, as said below
- first_local: int32 [128], P('pair'), may hold values from 0 to 3
- second_owner: int32 [128, 1], P('pair'), may hold values from 0 to 15; in each aligned block of 8 rows (0 to 7, 8 to 15, ...) at most 2 rows name the same one
- second_local: int32 [128], P('pair'), may hold values from 0 to 3
Outputs:
- new_log_depth: float32 [64, 196608], P('pair', 'img')
- new_moment_one: float32 [64, 196608], P('pair', 'img')
- new_moment_two: float32 [64, 196608], P('pair', 'img')
- pair_scale: float32 [128], P('pair')
Inputs may be any that keep to these rules, and one draw needn't show every extreme that they name: `second_owner`: among the 8 rows of one index of pair, no owner is named more than 2 times. `image_pose`: row 0 lies in 1 to 2. `pair_pose`: row 0 lies in 1 to 2.
All inputs are finite; a program needn't handle non-finite values.
Results may differ from a plain program's by a relative error of at most 0.0003.
The roundings to bfloat16 on the way count: a program that leaves them out, or rounds other values in their place, can miss the bound.
Values may be sent and summed in bfloat16 or wider, within the bound.
A program may use at most 128 MiB of HBM per device.

v0:
```python
import jax
import jax.numpy as jnp
from jax import lax
from jax.sharding import PartitionSpec as P

ROWS = 384
COLS = 512
ITERS = 3
START = 100


beta_one = 0.9
beta_two = 0.999
learn_rate = 0.01
adam_eps = 1e-08


def ray_dirs(pixels):
    row_pos = (pixels // COLS).astype(jnp.float32)
    col_pos = (pixels % COLS).astype(jnp.float32)
    return ((col_pos + 0.5 - COLS / 2) / COLS, (row_pos + 0.5 - ROWS / 2) / COLS)


def rotation(scalar_q, vec_a, vec_b, vec_c):
    magnitude = jnp.sqrt(scalar_q * scalar_q + vec_a * vec_a + vec_b * vec_b + vec_c * vec_c)
    unit_s = scalar_q / magnitude
    unit_a = vec_a / magnitude
    unit_b = vec_b / magnitude
    unit_c = vec_c / magnitude
    return (
        (
            1 - 2 * (unit_b * unit_b + unit_c * unit_c),
            2 * (unit_a * unit_b - unit_s * unit_c),
            2 * (unit_a * unit_c + unit_s * unit_b),
        ),
        (
            2 * (unit_a * unit_b + unit_s * unit_c),
            1 - 2 * (unit_a * unit_a + unit_c * unit_c),
            2 * (unit_b * unit_c - unit_s * unit_a),
        ),
        (
            2 * (unit_a * unit_c - unit_s * unit_b),
            2 * (unit_b * unit_c + unit_s * unit_a),
            1 - 2 * (unit_a * unit_a + unit_b * unit_b),
        ),
    )


def rigid_map(coords, pose_cols):
    matrix = rotation(pose_cols[0], pose_cols[1], pose_cols[2], pose_cols[3])
    rotated = [
        matrix[coord_id][0] * coords[0]
        + matrix[coord_id][1] * coords[1]
        + matrix[coord_id][2] * coords[2]
        for coord_id in range(3)
    ]
    placed = [rotated[coord_id] + pose_cols[4 + coord_id] for coord_id in range(3)]
    return (placed, rotated)


def world_points(rows_f, pose_cols, ray_x, ray_y):
    depths = jnp.exp(rows_f)
    return rigid_map((depths * ray_x, depths * ray_y, depths), pose_cols)


def pixel_sums(values):
    return lax.psum(values, "img")


def adam_update(log_depth, moment_one, moment_two, gradient, sweep):
    step_count = START + sweep + 1
    moment_one = beta_one * moment_one + (1 - beta_one) * gradient
    moment_two = beta_two * moment_two + (1 - beta_two) * gradient * gradient
    corrected_one = moment_one / (1 - beta_one**step_count)
    corrected_two = moment_two / (1 - beta_two**step_count)
    log_depth = log_depth - learn_rate * corrected_one / (jnp.sqrt(corrected_two) + adam_eps)
    return (log_depth, moment_one, moment_two)


def shards(
    log_depth,
    moment_one,
    moment_two,
    image_pose,
    pair_points,
    confidence,
    pair_pose,
    first_local,
    second_owner,
    second_local,
):
    img_dev = log_depth.shape[0]
    band_len = log_depth.shape[1]
    pair_dev = pair_points.shape[0]
    owners = lax.axis_size("pair")
    mine_index = lax.axis_index("pair")
    highest = lax.Precision.HIGHEST
    pixels = lax.axis_index("img") * band_len + jnp.arange(band_len, dtype=jnp.int32)
    ray_x, ray_y = ray_dirs(pixels)
    own_owner = second_owner[:, 0]
    local_ids = jnp.arange(img_dev, dtype=jnp.int32)
    image_ids = jnp.arange(img_dev * owners, dtype=jnp.int32)
    first_global = mine_index * img_dev + first_local
    second_global = own_owner * img_dev + second_local
    first_hot = (first_local[:, None] == local_ids[None, :]).astype(jnp.float32)
    first_pick = first_hot.astype(jnp.bfloat16)
    pose_first = jnp.dot(
        image_pose,
        (image_ids[:, None] == first_global[None, :]).astype(jnp.float32),
        precision=highest,
    )
    pose_second = jnp.dot(
        image_pose,
        (image_ids[:, None] == second_global[None, :]).astype(jnp.float32),
        precision=highest,
    )
    cols_first = [pose_first[k][:, None] for k in range(7)]
    cols_second = [pose_second[k][:, None] for k in range(7)]
    raw = pair_points.astype(jnp.float32).reshape(pair_dev, 2, 3, band_len)
    aligned_list, unused = rigid_map(
        (raw[:, :, 0], raw[:, :, 1], raw[:, :, 2]), [pair_pose[k][:, None, None] for k in range(7)]
    )
    aligned = jnp.stack(aligned_list, axis=2)
    weights = confidence.astype(jnp.float32)
    denominator = lax.psum(
        jnp.sum(weights * jnp.sum(aligned * aligned, axis=2), axis=(1, 2)), "img"
    )
    pair_scale = jnp.zeros((pair_dev,), jnp.float32)
    for sweep in range(ITERS):
        shared = lax.optimization_barrier(log_depth.astype(jnp.bfloat16))
        first_rows = jnp.dot(first_pick, shared, preferred_element_type=jnp.float32)
        block_rows = lax.all_gather(shared, "pair", axis=0, tiled=True)
        chosen = (
            second_global[:, None] == jnp.arange(block_rows.shape[0], dtype=jnp.int32)[None, :]
        ).astype(jnp.bfloat16)
        second_rows = jnp.dot(chosen, block_rows, preferred_element_type=jnp.float32)
        world_one, lever_one = world_points(first_rows, cols_first, ray_x, ray_y)
        world_two, lever_two = world_points(second_rows, cols_second, ray_x, ray_y)
        world = jnp.stack([jnp.stack(world_one, axis=1), jnp.stack(world_two, axis=1)], axis=1)
        levers = jnp.stack([jnp.stack(lever_one, axis=1), jnp.stack(lever_two, axis=1)], axis=1)
        numerator = pixel_sums(jnp.sum(weights * jnp.sum(world * aligned, axis=2), axis=(1, 2)))
        pair_scale = numerator / denominator
        residual = world - pair_scale[:, None, None, None] * aligned
        gradient_pairs = 2.0 * weights * jnp.sum(residual * levers, axis=2)
        gradient = jnp.dot(first_hot.T, gradient_pairs[:, 0], precision=highest)
        second_terms = gradient_pairs[:, 1]
        image_chosen = (
            jnp.arange(img_dev * lax.axis_size("pair"), dtype=jnp.int32)[:, None]
            == second_global[None, :]
        ).astype(jnp.float32)
        gradient = gradient + lax.psum_scatter(
            jnp.dot(image_chosen, second_terms, precision=highest),
            "pair",
            scatter_dimension=0,
            tiled=True,
        )
        log_depth, moment_one, moment_two = adam_update(
            log_depth, moment_one, moment_two, gradient, sweep
        )
    return (log_depth, moment_one, moment_two, pair_scale)


def solution(mesh):
    return jax.shard_map(
        shards,
        mesh=mesh,
        in_specs=(
            P("pair", "img"),
            P("pair", "img"),
            P("pair", "img"),
            P(),
            P("pair", None, "img"),
            P("pair", None, "img"),
            P(None, "pair"),
            P("pair"),
            P("pair", None),
            P("pair"),
        ),
        out_specs=(P("pair", "img"), P("pair", "img"), P("pair", "img"), P("pair")),
        check_vma=False,
    )
```

profile of v0, /device:TPU:1, one launch (start us, length us, event | category | flops | bytes accessed | tf_op | source)
XLA Modules:
  0.0 657.0 jit_solution(18423964423283320140)
XLA Ops:
  25.3 36.5 %all-gather.7.cloned.1.call-done = bf16[16,4,24576]{2,1,0:T(4,128)(2,1)} async-done(((bf16[1,4,24576]{2,1,0:T(4,128)(2,1)}), bf16[16,4,24576]{2,1,0:T(4,128)(2,1)}) %all-gather.7.cloned.1.call-update) | async-done | bytes 3145744 | tf_op jit(solution)/shard_map/all_gather | solution.py:132
  61.8 4.5 reshape.969
  66.4 4.3 add_bitcast_fusion.14
  76.0 12.7 %all-reduce.3 = (f32[8]{0:T(128)S(1)}, f32[8]{0:T(128)S(1)}) all-reduce(f32[8]{0:T(128)S(1)} %get-tuple-element.7, f32[8]{0:T(128)S(1)} %get-tuple-element.6), channel_id=1, replica_groups=mesh['img'=8,'pair'=16] {'img'}, use_global_device_ids=true, to_apply=%region_2.3 | all-reduce | flops 16 | bytes 128 | tf_op jit(solution)/shard_map/psum | solution.py:67
  91.7 3.0 fusion
  96.4 4.4 fusion.12
  102.8 118.6 %all-reduce.8.cloned.1.call-done = f32[64,24576]{1,0:T(8,128)} async-done(((f32[64,24576]{1,0:T(8,128)}), f32[64,24576]{1,0:T(8,128)}) %all-reduce.8.cloned.1.call-update) | async-done | bytes 6291472
  221.4 3.8 fusion.73
  225.6 3.1 add_bitcast_fusion.11
  230.3 42.6 %all-gather.9.cloned.1.call-done = bf16[16,4,24576]{2,1,0:T(4,128)(2,1)} async-done(((bf16[1,4,24576]{2,1,0:T(4,128)(2,1)}), bf16[16,4,24576]{2,1,0:T(4,128)(2,1)}) %all-gather.9.cloned.1.call-update) | async-done | bytes 3145744 | tf_op jit(solution)/shard_map/all_gather | solution.py:132
  272.9 4.5 reshape.971
  277.4 4.4 add_bitcast_fusion.8
  288.8 12.7 %psum.30 = f32[8]{0:T(128)S(1)} all-reduce(f32[8]{0:T(128)S(1)} %fusion.8), channel_id=1, replica_groups=mesh['img'=8,'pair'=16] {'img'}, use_global_device_ids=true, to_apply=%region_10.11 | all-reduce | flops 8 | bytes 64 | tf_op jit(solution)/shard_map/psum | solution.py:67
  309.1 4.4 fusion.11
  313.6 120.5 %all-reduce.10.cloned.1.call-done = f32[64,24576]{1,0:T(8,128)} async-done(((f32[64,24576]{1,0:T(8,128)}), f32[64,24576]{1,0:T(8,128)}) %all-reduce.10.cloned.1.call-update) | async-done | bytes 6291472
  434.1 4.1 fusion.72
  438.3 3.1 add_bitcast_fusion.5
  443.1 42.8 %all-gather.11.cloned.1.call-done = bf16[16,4,24576]{2,1,0:T(4,128)(2,1)} async-done(((bf16[1,4,24576]{2,1,0:T(4,128)(2,1)}), bf16[16,4,24576]{2,1,0:T(4,128)(2,1)}) %all-gather.11.cloned.1.call-update) | async-done | bytes 3145744 | tf_op jit(solution)/shard_map/all_gather | solution.py:132
  485.9 4.5 reshape.973
  490.4 4.4 add_bitcast_fusion.2
  501.8 12.9 %psum.31 = f32[8]{0:T(128)S(1)} all-reduce(f32[8]{0:T(128)S(1)} %fusion.9), channel_id=1, replica_groups=mesh['img'=8,'pair'=16] {'img'}, use_global_device_ids=true, to_apply=%region_15.16 | all-reduce | flops 8 | bytes 64 | tf_op jit(solution)/shard_map/psum | solution.py:67
  521.2 4.4 fusion.10
  525.7 120.5 %all-reduce.12.cloned.1.call-done = f32[64,24576]{1,0:T(8,128)} async-done(((f32[64,24576]{1,0:T(8,128)}), f32[64,24576]{1,0:T(8,128)}) %all-reduce.12.cloned.1.call-update) | async-done | bytes 6291472
  646.2 3.9 divide_subtract_fusion
  (199 shorter events, 60.7 us)
Async XLA Ops:
  7.2 5.3 copy-start
  7.2 54.7 %all-gather.7.cloned.1.call-start = ((), (), s32[]{:S(2)}) async-start(), calls=%async_computation | async-start | bytes 3342336 | tf_op jit(solution)/shard_map/all_gather | solution.py:132
  9.0 212.4 %all-reduce.8.cloned.1.call-start = ((), (), s32[]{:S(2)}) async-start(), calls=%async_computation.3 | async-start | bytes 12582912
  25.3 41.0 %copy-start.34 = (f32[8]{0:T(128)S(1)}, f32[8]{0:T(128)}, u32[]{:S(2)}) copy-start(f32[8]{0:T(128)} %get-tuple-element.31) | copy-start | bytes 100
  25.3 41.0 %copy-start.37 = (f32[8]{0:T(128)S(1)}, f32[8]{0:T(128)}, u32[]{:S(2)}) copy-start(f32[8]{0:T(128)} %get-tuple-element.35) | copy-start | bytes 100
  70.8 4.1 copy-start.20
  100.8 120.6 %copy-start.55 = (s32[8]{0:T(128)S(1)}, s32[8]{0:T(128)}, u32[]{:S(2)}) copy-start(s32[8]{0:T(128)} %param.17) | copy-start | bytes 100
  100.8 172.0 %all-gather.9.cloned.1.call-start = ((), (), s32[]{:S(2)}) async-start(), calls=%async_computation.1 | async-start | bytes 3342336 | tf_op jit(solution)/shard_map/all_gather | solution.py:132
  102.7 122.8 %copy-start.33 = (f32[8]{0:T(128)S(1)}, f32[8]{0:T(128)}, u32[]{:S(2)}) copy-start(f32[8]{0:T(128)} %get-tuple-element.105) | copy-start | bytes 100
  102.7 122.8 %copy-start.36 = (f32[8]{0:T(128)S(1)}, f32[8]{0:T(128)}, u32[]{:S(2)}) copy-start(f32[8]{0:T(128)} %get-tuple-element.24) | copy-start | bytes 100
  102.7 122.8 %copy-start.39 = (f32[8]{0:T(128)S(1)}, f32[8]{0:T(128)}, u32[]{:S(2)}) copy-start(f32[8]{0:T(128)} %copy-done.38) | copy-start | bytes 100
  102.7 122.8 %copy-start.41 = (f32[8]{0:T(128)S(1)}, f32[8]{0:T(128)}, u32[]{:S(2)}) copy-start(f32[8]{0:T(128)} %copy-done.40) | copy-start | bytes 100
  102.7 122.8 %copy-start.43 = (f32[8]{0:T(128)S(1)}, f32[8]{0:T(128)}, u32[]{:S(2)}) copy-start(f32[8]{0:T(128)} %copy-done.42) | copy-start | bytes 100
  102.7 122.8 %copy-start.45 = (f32[8]{0:T(128)S(1)}, f32[8]{0:T(128)}, u32[]{:S(2)}) copy-start(f32[8]{0:T(128)} %copy-done.44) | copy-start | bytes 100
  102.8 122.8 %copy-start.47 = (f32[8]{0:T(128)S(1)}, f32[8]{0:T(128)}, u32[]{:S(2)}) copy-start(f32[8]{0:T(128)} %copy-done.46) | copy-start | bytes 100
  102.8 122.8 %copy-start.49 = (f32[8]{0:T(128)S(1)}, f32[8]{0:T(128)}, u32[]{:S(2)}) copy-start(f32[8]{0:T(128)} %copy-done.48) | copy-start | bytes 100
  102.8 122.8 %copy-start.51 = (f32[8]{0:T(128)S(1)}, f32[8]{0:T(128)}, u32[]{:S(2)}) copy-start(f32[8]{0:T(128)} %copy-done.50) | copy-start | bytes 100
  102.8 122.8 %copy-start.53 = (f32[8]{0:T(128)S(1)}, f32[8]{0:T(128)}, u32[]{:S(2)}) copy-start(f32[8]{0:T(128)} %copy-done.52) | copy-start | bytes 100
  225.2 208.9 %all-reduce.10.cloned.1.call-start = ((), (), s32[]{:S(2)}) async-start(), calls=%async_computation.4 | async-start | bytes 12582912
  313.6 172.3 %all-gather.11.cloned.1.call-start = ((), (), s32[]{:S(2)}) async-start(), calls=%async_computation.2 | async-start | bytes 3342336 | tf_op jit(solution)/shard_map/all_gather | solution.py:132
  438.2 208.0 %all-reduce.12.cloned.1.call-start = ((), (), s32[]{:S(2)}) async-start(), calls=%async_computation.5 | async-start | bytes 12582912
  525.6 120.6 %copy-start.65 = (f32[4,24576]{1,0:T(4,128)S(1)}, f32[4,24576]{1,0:T(4,128)}, u32[]{:S(2)}) copy-start(f32[4,24576]{1,0:T(4,128)} %param.12) | copy-start | bytes 1179652
  525.6 120.6 %copy-start.66 = (f32[4,24576]{1,0:T(4,128)S(1)}, f32[4,24576]{1,0:T(4,128)}, u32[]{:S(2)}) copy-start(f32[4,24576]{1,0:T(4,128)} %param.11) | copy-start | bytes 1179652
  525.6 120.6 %copy-start.68 = (f32[4,24576]{1,0:T(4,128)S(1)}, f32[4,24576]{1,0:T(4,128)}, u32[]{:S(2)}) copy-start(f32[4,24576]{1,0:T(4,128)} %get-tuple-element.130) | copy-start | bytes 1179652
  (51 other events, 97.7 us)
Sparse Core Ops, SparseCore 0:
  10.8 51.0 all-gather.6
  101.0 120.3 all-reduce.7
  225.3 47.4 all-gather.8
  313.7 120.3 all-reduce.9
  438.4 47.4 all-gather.10
  525.8 120.3 all-reduce.11
where the time goes:
time: 658 us; the launch traced here: 657 us
  waiting for transfers between devices  482 us (73%)
  matrix products  45.5 us (7%)
  other arithmetic  43.1 us (7%)
  blocking collectives  38.4 us (6%)
  local copies, waits for them, and re-layouts  32.5 us (5%)
  between operations  15.4 us (2%)
    unnamed x9, waiting for transfers between devices  360 us
    all_gather x3, waiting for transfers between devices, shards(): block_rows = lax.all_gather(shared, 'pair', axis=0, tiled=True)  122 us
    psum x3, blocking collectives, pixel_sums(): return lax.psum(values, 'img')  38.4 us
    unnamed x142, local copies, waits for them, and re-layouts  30.6 us
    dot_general x3, matrix products, shards(): jnp.dot(image_chosen, second_terms, precision=highest)  13.3 us
  transfers between devices with their start and end apart: 6, of which 6 were waited for; matrix products, arithmetic and copies ran while one was open for 4% of the time, Pallas kernels for 0%

commit v1 on v0

v1 whole, which is shorter than its diff:
```python
import jax
import jax.numpy as jnp
from jax import lax
from jax.experimental import pallas as pl
from jax.experimental.pallas import tpu as pltpu
from jax.sharding import PartitionSpec as P

ROWS = 384
COLS = 512
ITERS = 3
START = 100
IMG_DEV = 4
PAIR_DEV = 8
MOST = 2
IMGS = 8
OWNERS = 16
YS = 4
ZS = 4
BAND = ROWS * COLS // IMGS
GROUPS = BAND // 128
BLOCKS = GROUPS // 8
BAND_ROWS = ROWS // IMGS
SLOTS = OWNERS * MOST
VIEWS = PAIR_DEV + SLOTS
CODE_ROWS = 2 * GROUPS + 16
TILE = 4
LEVELS = 32700.0
SCALE_STEPS = 64.0

beta_one = 0.9
beta_two = 0.999
learn_rate = 0.01
adam_eps = 1e-08
f32 = jnp.float32
MESH = pl.DeviceIdType.MESH


def rotation(scalar_q, vec_a, vec_b, vec_c):
    magnitude = jnp.sqrt(scalar_q * scalar_q + vec_a * vec_a + vec_b * vec_b + vec_c * vec_c)
    unit_s = scalar_q / magnitude
    unit_a = vec_a / magnitude
    unit_b = vec_b / magnitude
    unit_c = vec_c / magnitude
    return (
        (
            1 - 2 * (unit_b * unit_b + unit_c * unit_c),
            2 * (unit_a * unit_b - unit_s * unit_c),
            2 * (unit_a * unit_c + unit_s * unit_b),
        ),
        (
            2 * (unit_a * unit_b + unit_s * unit_c),
            1 - 2 * (unit_a * unit_a + unit_c * unit_c),
            2 * (unit_b * unit_c - unit_s * unit_a),
        ),
        (
            2 * (unit_a * unit_c - unit_s * unit_b),
            2 * (unit_b * unit_c + unit_s * unit_a),
            1 - 2 * (unit_a * unit_a + unit_b * unit_b),
        ),
    )


def kernel(
    log_ref,
    one_ref,
    two_ref,
    points_ref,
    conf_ref,
    image_pose,
    pair_pose,
    first_local,
    second_owner,
    second_local,
    log_out,
    one_out,
    two_out,
    scale_out,
    conf_f,
    stage_one,
    stage_two,
    codes,
    send_buf,
    recv_buf,
    meta,
    cu_ref,
    weight_sum,
    depth_ref,
    tau_ref,
    hot_ref,
    mask_ref,
    weight_ref,
    inner_ref,
    img_buf,
    pair_buf,
    image_tab,
    send_sem,
    recv_sem,
    meta_send,
    meta_recv,
    img_send,
    img_recv,
    pair_send,
    pair_recv,
):
    my_img = lax.axis_index("img")
    my_pair = lax.axis_index("pair")
    my_y = my_pair // ZS
    my_z = my_pair % ZS

    def pair_at(k, sign):
        return ((my_y + sign * (k // ZS) + YS) % YS) * ZS + (my_z + sign * (k % ZS) + ZS) % ZS

    barrier = pltpu.get_barrier_semaphore()

    def greet_pair(k, carry):
        pl.semaphore_signal(barrier, 1, device_id=(my_img, pair_at(k, -1)), device_id_type=MESH)
        return carry

    def greet_img(k, carry):
        pl.semaphore_signal(barrier, 1, device_id=((my_img + k) % IMGS, my_pair), device_id_type=MESH)
        return carry

    lax.fori_loop(1, OWNERS, greet_pair, 0)
    lax.fori_loop(1, IMGS, greet_img, 0)

    sub = lax.broadcasted_iota(jnp.int32, (8, 128), 0)
    lane = lax.broadcasted_iota(jnp.int32, (8, 128), 1)

    owners = [second_owner[e] for e in range(PAIR_DEV)]
    order = []
    for e in range(PAIR_DEV):
        rank = jnp.int32(0)
        for other in range(e):
            rank = rank + jnp.where(owners[other] == owners[e], 1, 0)
        order.append(owners[e] * MOST + rank)
    row = jnp.zeros((8, 128), jnp.int32)
    for e in range(PAIR_DEV):
        here = lane == my_pair * PAIR_DEV + e
        row = jnp.where(here & (sub == 0), order[e], row)
        row = jnp.where(here & (sub == 1), second_local[e], row)
    meta[0] = row

    def column(values):
        out = jnp.zeros((8, 128), f32)
        for e in range(PAIR_DEV):
            out = jnp.where(sub == e, values[e], out)
        return out

    pair_cols = [column([pair_pose[i, e] for e in range(PAIR_DEV)]) for i in range(7)]
    pair_rot = rotation(*pair_cols[:4])
    shift = pair_cols[4:]
    firsts = [my_pair * IMG_DEV + first_local[e] for e in range(PAIR_DEV)]
    seconds = [owners[e] * IMG_DEV + second_local[e] for e in range(PAIR_DEV)]
    lean = [2.0 * sum(pair_rot[i][j] * shift[i] for i in range(3)) for j in range(3)]
    shift_sq = sum(shift[i] * shift[i] for i in range(3))
    first_row = (my_img * BAND_ROWS).astype(f32)
    ray_y0 = (first_row + 0.5 - ROWS / 2) / COLS
    ray_x = [((lane + 128 * part).astype(f32) + 0.5 - COLS / 2) / COLS for part in range(4)]

    def widen(step, carry):
        rows = pl.ds(pl.multiple_of(step * 64, 64), 64)
        conf_f[rows, :] = conf_ref[rows, :].astype(f32)
        return carry

    lax.fori_loop(0, PAIR_DEV * 2 * GROUPS // 64, widen, 0)

    def prepare(view, images, stage, scaled):
        cols = [column([image_pose[i, images[e]] for e in range(PAIR_DEV)]) for i in range(7)]
        rot = rotation(*cols[:4])
        trans = cols[4:]
        both = [[sum(rot[l][i] * pair_rot[l][j] for l in range(3)) for j in range(3)] for i in range(3)]
        moved = [sum(rot[l][i] * shift[l] for l in range(3)) for i in range(3)]
        full = [[both[i][0], both[i][1], both[i][2], moved[i]] for i in range(3)]
        base = [[ray_x[part] * full[0][j] + (full[2][j] + ray_y0 * full[1][j]) for part in range(4)] for j in range(4)]
        slope = [full[1][j] * (1.0 / COLS) for j in range(4)]
        toward = [sum(trans[l] * pair_rot[l][j] for l in range(3)) for j in range(3)]
        offset = sum(trans[l] * shift[l] for l in range(3))

        def body(r, carry):
            total_sq, total_dot, total_conf = carry
            down = r.astype(f32)
            tilt = [slope[j] * down for j in range(4)]
            for part in range(4):
                at = pl.ds(pl.multiple_of(r * COLS + part * 128, 128), 128)
                x = [points_ref[3 * view + j, :, at].astype(f32) for j in range(3)]
                weight = conf_f[pl.ds((r * 4 + part) * 2 + view, 8, stride=2 * GROUPS), :]
                value = base[3][part] + tilt[3]
                for j in range(3):
                    value = value + (base[j][part] + tilt[j]) * x[j]
                if scaled:
                    value = value * weight
                stage[pl.ds(pl.multiple_of((r * 4 + part) * 8, 8), 8), :] = value
                square = x[0] * (x[0] + lean[0]) + x[1] * (x[1] + lean[1]) + x[2] * (x[2] + lean[2])
                dot = x[0] * toward[0] + x[1] * toward[1] + x[2] * toward[2]
                total_sq = total_sq + weight * square
                total_dot = total_dot + weight * dot
                total_conf = total_conf + weight
            return (total_sq, total_dot, total_conf)

        zero = jnp.zeros((8, 128), f32)
        total_sq, total_dot, total_conf = lax.fori_loop(0, BAND_ROWS, body, (zero, zero, zero))
        return (total_sq + total_conf * shift_sq, total_dot + total_conf * offset)

    square_two, dot_two = prepare(1, seconds, stage_two, False)

    def encode(e, carry):
        largest = jnp.full((8, 128), 1e-30, f32)
        for block in range(BLOCKS):
            largest = jnp.maximum(largest, jnp.abs(stage_two[pl.ds(block * 64 + e, 8, stride=8), :]))
        power = jnp.ceil(jnp.log(largest) * (SCALE_STEPS / 0.6931471805599453)).astype(jnp.int32)
        inverse = LEVELS / jnp.exp(power.astype(f32) * (0.6931471805599453 / SCALE_STEPS))
        inverse = jnp.concatenate([inverse, inverse], axis=0)
        for half in range(BLOCKS // 2):
            value = stage_two[pl.ds(half * 128 + e, 16, stride=8), :] * inverse
            value = jnp.floor(value + 0.5).astype(jnp.int32).astype(jnp.int16)
            codes[e, half * 16 : half * 16 + 16, :] = value
            weight = conf_f[pl.ds(e * 2 * GROUPS + half * 32 + 1, 16, stride=2), :] * 128.0
            codes[e, GROUPS + half * 16 : GROUPS + half * 16 + 16, :] = weight.astype(jnp.int32).astype(jnp.int16)
        codes[e, 2 * GROUPS : 2 * GROUPS + 16, :] = jnp.concatenate([power, power], axis=0).astype(jnp.int16)
        return carry

    lax.fori_loop(0, PAIR_DEV, encode, 0)

    def slot_pair(k, j):
        wanted = pair_at(k, 1) * MOST + j
        found = jnp.int32(0)
        for e in range(1, PAIR_DEV):
            found = found + jnp.where(order[e] == wanted, e, 0)
        return found

    for j in range(MOST):
        recv_buf[0, j] = codes[slot_pair(0, j)]

    pl.semaphore_wait(barrier, OWNERS - 1 + IMGS - 1)

    def meta_copy(k):
        return pltpu.make_async_remote_copy(
            src_ref=meta.at[0],
            dst_ref=meta.at[k],
            send_sem=meta_send.at[k],
            recv_sem=meta_recv.at[k],
            device_id=(my_img, pair_at(k, 1)),
            device_id_type=MESH,
        )

    def slot_copy(k):
        return pltpu.make_async_remote_copy(
            src_ref=send_buf.at[k],
            dst_ref=recv_buf.at[k],
            send_sem=send_sem.at[k],
            recv_sem=recv_sem.at[k],
            device_id=(my_img, pair_at(k, 1)),
            device_id_type=MESH,
        )

    def start_meta(k, carry):
        meta_copy(k).start()
        return carry

    def start_slots(k, carry):
        for j in range(MOST):
            send_buf[k, j] = codes[slot_pair(k, j)]
        slot_copy(k).start()
        return carry

    lax.fori_loop(1, OWNERS, start_meta, 0)
    lax.fori_loop(1, OWNERS, start_slots, 0)

    square_one, dot_one = prepare(0, firsts, stage_one, True)

    def depth_of(values):
        return jnp.exp(values.astype(jnp.bfloat16).astype(f32))

    def image_rows(block, v):
        return pl.ds(block * 32 + v, 8, stride=IMG_DEV)

    def block_rows(block):
        return pl.ds(pl.multiple_of(block * 8, 8), 8)

    def first_depth(block, carry):
        for v in range(IMG_DEV):
            depth_ref[v, block_rows(block), :] = depth_of(log_ref[image_rows(block, v), :])
        return carry

    lax.fori_loop(0, BLOCKS, first_depth, 0)

    own = [[image_pose[i, my_pair * IMG_DEV + min(v, IMG_DEV - 1)] for v in range(8)] for i in range(7)]
    own_cols = [column(own[i]) for i in range(7)]
    own_rot = rotation(*own_cols[:4])
    for i in range(3):
        tau_ref[i] = sum(own_rot[l][i] * own_cols[4 + l] for l in range(3))

    for k in range(1, OWNERS):
        meta_copy(k).wait_recv()
    known = meta[0]
    for k in range(1, OWNERS):
        known = known + meta[k]
    code_row = jnp.broadcast_to(known[0:1], (8, 128))
    local_row = jnp.broadcast_to(known[1:2], (8, 128))
    from_pair = lane // PAIR_DEV
    step_of = ((my_y - from_pair // ZS + YS) % YS) * ZS + (my_z - from_pair % ZS + ZS) % ZS
    slot_of = jnp.where(code_row // MOST == my_pair, step_of * MOST + code_row % MOST, -1)
    local_first = jnp.zeros((8, 128), jnp.int32)
    for e in range(PAIR_DEV):
        local_first = jnp.where(sub == e, first_local[e], local_first)
    own_mask = jnp.where(lane == my_pair * PAIR_DEV + sub, 1.0, 0.0)
    mask_ref[0:8, :] = own_mask
    for v in range(IMG_DEV):
        hot_ref[v, 0:8, :] = jnp.where(local_first == v, 1.0, 0.0)
    for group in range(SLOTS // 8):
        rows = pl.ds(8 + group * 8, 8)
        held = slot_of == sub + group * 8
        mask_ref[rows, :] = jnp.where(held, 1.0, 0.0)
        for v in range(IMG_DEV):
            found = jnp.where(held & (local_row == v), 1.0, 0.0)
            hot_ref[v, rows, :] = jnp.broadcast_to(jnp.sum(found, axis=1, keepdims=True), (8, 128))
    for e in range(PAIR_DEV):
        image_tab[e] = first_local[e]

    def find_image(r, carry):
        image_tab[PAIR_DEV + r] = jnp.sum(jnp.where((slot_of == r) & (sub == 0), local_row, 0))
        return carry

    lax.fori_loop(0, SLOTS, find_image, 0)

    def first_cu(e, block):
        return stage_one[pl.ds(block * 64 + e, 8, stride=8), :]

    def dot_first(e, carry):
        v = image_tab[e]
        total = jnp.zeros((8, 128), f32)
        for block in range(BLOCKS):
            total = total + first_cu(e, block) * depth_ref[v, block * 8 : block * 8 + 8, :]
        inner_ref[pl.ds(e, 1), :] = jnp.sum(total, axis=0, keepdims=True)
        return carry

    def dot_second(r, carry):
        v = image_tab[PAIR_DEV + r]
        total = jnp.zeros((8, 128), f32)
        for block in range(BLOCKS):
            total = total + cu_ref[r, block * 8 : block * 8 + 8, :] * depth_ref[v, block * 8 : block * 8 + 8, :]
        inner_ref[pl.ds(PAIR_DEV + r, 1), :] = jnp.sum(total, axis=0, keepdims=True)
        return carry

    lax.fori_loop(0, PAIR_DEV, dot_first, 0)

    def first_sums(block, carry):
        sums = [jnp.zeros((8, 128), f32) for v in range(IMG_DEV)]
        for e in range(PAIR_DEV):
            weight = conf_f[pl.ds(e * 2 * GROUPS + block * 16, 8, stride=2), :]
            for v in range(IMG_DEV):
                sums[v] = sums[v] + weight * hot_ref[v, e : e + 1, :]
        for v in range(IMG_DEV):
            weight_sum[v, block_rows(block), :] = sums[v]
        return carry

    lax.fori_loop(0, BLOCKS, first_sums, 0)

    def take(k, carry):
        @pl.when(k > 0)
        def _():
            slot_copy(k).wait_recv()

        units, hots, images = [], [], []
        for j in range(MOST):
            power = recv_buf[k, j, 2 * GROUPS : 2 * GROUPS + 16, :].astype(jnp.int32).astype(f32)
            unit = jnp.exp(power * (0.6931471805599453 / SCALE_STEPS)) * (1.0 / (LEVELS * 128.0))
            units.append(unit)
            slot = PAIR_DEV + k * MOST + j
            hots.append([hot_ref[v, pl.ds(slot, 1), :] * (1.0 / 128.0) for v in range(IMG_DEV)])
            images.append(image_tab[slot])

        def part(half, totals):
            totals = list(totals)
            rows = pl.ds(pl.multiple_of(half * 16, 16), 16)
            weight_rows = pl.ds(pl.multiple_of(GROUPS + half * 16, 16), 16)
            sums = [weight_sum[v, rows, :] for v in range(IMG_DEV)]
            for j in range(MOST):
                value = recv_buf[k, j, rows, :].astype(jnp.int32).astype(f32)
                weight = recv_buf[k, j, weight_rows, :].astype(jnp.int32).astype(f32)
                cu = value * units[j] * weight
                cu_ref[k * MOST + j, rows, :] = cu
                totals[j] = totals[j] + cu * depth_ref[images[j], rows, :]
                for v in range(IMG_DEV):
                    sums[v] = sums[v] + weight * hots[j][v]
            for v in range(IMG_DEV):
                weight_sum[v, rows, :] = sums[v]
            return tuple(totals)

        totals = lax.fori_loop(0, BLOCKS // 2, part, tuple(jnp.zeros((16, 128), f32) for j in range(MOST)))
        for j in range(MOST):
            inner_ref[pl.ds(PAIR_DEV + k * MOST + j, 1), :] = jnp.sum(totals[j], axis=0, keepdims=True)
        return carry

    lax.fori_loop(0, OWNERS, take, 0)

    def pair_row(col):
        return jnp.sum(jnp.sum(col, axis=1, keepdims=True) * own_mask, axis=0, keepdims=True)

    fixed_row = pair_row(dot_one + dot_two)
    square_row = pair_row(square_one + square_two)

    def img_copy(t, k):
        return pltpu.make_async_remote_copy(
            src_ref=img_buf.at[t, my_img],
            dst_ref=img_buf.at[t, my_img],
            send_sem=img_send.at[t, k],
            recv_sem=img_recv.at[t, my_img],
            device_id=((my_img + k) % IMGS, my_pair),
            device_id_type=MESH,
        )

    def img_arrival(t, k):
        source = (my_img + k) % IMGS
        return pltpu.make_async_remote_copy(
            src_ref=img_buf.at[t, source],
            dst_ref=img_buf.at[t, source],
            send_sem=img_send.at[t, k],
            recv_sem=img_recv.at[t, source],
            device_id=(source, my_pair),
            device_id_type=MESH,
        )

    def pair_copy(t, k):
        return pltpu.make_async_remote_copy(
            src_ref=pair_buf.at[t, my_pair],
            dst_ref=pair_buf.at[t, my_pair],
            send_sem=pair_send.at[t, k],
            recv_sem=pair_recv.at[t, my_pair],
            device_id=(my_img, pair_at(k, 1)),
            device_id_type=MESH,
        )

    def pair_arrival(t, k):
        source = pair_at(k, 1)
        return pltpu.make_async_remote_copy(
            src_ref=pair_buf.at[t, source],
            dst_ref=pair_buf.at[t, source],
            send_sem=pair_send.at[t, k],
            recv_sem=pair_recv.at[t, source],
            device_id=(my_img, source),
            device_id_type=MESH,
        )

    def sum_all(t, tile):
        img_buf[t, my_img] = tile
        for k in range(1, IMGS):
            img_copy(t, k).start()
        for k in range(1, IMGS):
            img_arrival(t, k).wait_recv()
        total = img_buf[t, 0]
        for k in range(1, IMGS):
            total = total + img_buf[t, k]
        pair_buf[t, my_pair] = total
        for k in range(1, OWNERS):
            pair_copy(t, k).start()
        for k in range(1, OWNERS):
            pair_arrival(t, k).wait_recv()
        total = pair_buf[t, 0]
        for k in range(1, OWNERS):
            total = total + pair_buf[t, k]
        return total

    denominator = None
    for sweep in range(ITERS):
        row = jnp.zeros((8, 128), f32)
        for group in range(VIEWS // 8):
            rows = slice(group * 8, group * 8 + 8)
            row = row + jnp.sum(inner_ref[rows, :], axis=1, keepdims=True) * mask_ref[rows, :]
        row = jnp.sum(row, axis=0, keepdims=True) + fixed_row
        tile = jnp.where(sub == 0, row, jnp.where(sub == 1, square_row, 0.0))
        total = sum_all(sweep, tile)
        if sweep == 0:
            denominator = total[1:2]
        scales = jnp.broadcast_to(total[0:1] / denominator, (8, 128))
        for group in range(VIEWS // 8):
            rows = slice(group * 8, group * 8 + 8)
            held = jnp.sum(scales * mask_ref[rows, :], axis=1, keepdims=True)
            if group == 0 and sweep == ITERS - 1:
                own_row = jnp.sum(jnp.where(lane == sub, held, 0.0), axis=0, keepdims=True)
                scale_out[...] = own_row[:, 0:PAIR_DEV]
            for v in range(IMG_DEV):
                weight_ref[v, rows, :] = held * hot_ref[v, rows, :]

        steps = START + sweep + 1
        bias_one = 1 - beta_one**steps
        bias_two = 1 - beta_two**steps
        last = sweep == ITERS - 1

        def update(tile_id, carry):
            start = tile_id * TILE

            def gather_first(e, sums):
                sums = list(sums)
                for n in range(TILE):
                    cu = first_cu(e, start + n)
                    for v in range(IMG_DEV):
                        sums[n * IMG_DEV + v] = sums[n * IMG_DEV + v] + cu * weight_ref[v, pl.ds(e, 1), :]
                return tuple(sums)

            def gather_second(r, sums):
                sums = list(sums)
                for n in range(TILE):
                    cu = cu_ref[r, block_rows(start + n), :]
                    for v in range(IMG_DEV):
                        sums[n * IMG_DEV + v] = sums[n * IMG_DEV + v] + cu * weight_ref[v, pl.ds(PAIR_DEV + r, 1), :]
                return tuple(sums)

            sums = tuple(jnp.zeros((8, 128), f32) for i in range(TILE * IMG_DEV))
            sums = lax.fori_loop(0, PAIR_DEV, gather_first, sums)
            sums = lax.fori_loop(0, SLOTS, gather_second, sums)
            for n in range(TILE):
                block = start + n
                down = (block * 2 + sub // 4).astype(f32) + first_row
                rays_y = (down + 0.5 - ROWS / 2) / COLS
                rays_x = (((sub % 4) * 128 + lane).astype(f32) + 0.5 - COLS / 2) / COLS
                length = rays_x * rays_x + rays_y * rays_y + 1.0
                for v in range(IMG_DEV):
                    depth = depth_ref[v, block_rows(block), :]
                    lever = rays_x * tau_ref[0, v : v + 1, :] + rays_y * tau_ref[1, v : v + 1, :] + tau_ref[2, v : v + 1, :]
                    pull = (depth * length + lever) * weight_sum[v, block_rows(block), :] - sums[n * IMG_DEV + v]
                    gradient = 2.0 * depth * pull
                    rows = image_rows(block, v)
                    old_one = (one_ref if sweep == 0 else one_out)[rows, :]
                    old_two = (two_ref if sweep == 0 else two_out)[rows, :]
                    old_log = (log_ref if sweep == 0 else log_out)[rows, :]
                    new_one = beta_one * old_one + (1 - beta_one) * gradient
                    new_two = beta_two * old_two + (1 - beta_two) * gradient * gradient
                    corrected_one = new_one * (1 / bias_one)
                    corrected_two = new_two * (1 / bias_two)
                    new_log = old_log - learn_rate * corrected_one / (jnp.sqrt(corrected_two) + adam_eps)
                    one_out[rows, :] = new_one
                    two_out[rows, :] = new_two
                    log_out[rows, :] = new_log
                    if not last:
                        depth_ref[v, block_rows(block), :] = depth_of(new_log)
            return carry

        lax.fori_loop(0, BLOCKS // TILE, update, 0)
        if not last:
            lax.fori_loop(0, PAIR_DEV, dot_first, 0)
            lax.fori_loop(0, SLOTS, dot_second, 0)

    def finish(k, carry):
        meta_copy(k).wait_send()
        slot_copy(k).wait_send()
        return carry

    lax.fori_loop(1, OWNERS, finish, 0)
    for t in range(ITERS):
        for k in range(1, IMGS):
            img_copy(t, k).wait_send()
        for k in range(1, OWNERS):
            pair_copy(t, k).wait_send()


def shards(
    log_depth,
    moment_one,
    moment_two,
    image_pose,
    pair_points,
    confidence,
    pair_pose,
    first_local,
    second_owner,
    second_local,
):
    def fold(a):
        return a.reshape(IMG_DEV, GROUPS, 128).transpose(1, 0, 2).reshape(GROUPS * IMG_DEV, 128)

    def unfold(a):
        return a.reshape(GROUPS, IMG_DEV, 128).transpose(1, 0, 2).reshape(IMG_DEV, BAND)

    points = pair_points.transpose(1, 0, 2)
    conf = confidence.reshape(PAIR_DEV, 2, GROUPS, 128).transpose(0, 2, 1, 3).reshape(PAIR_DEV * GROUPS * 2, 128)
    vmem = pl.BlockSpec(memory_space=pltpu.VMEM)
    smem = pl.BlockSpec(memory_space=pltpu.SMEM)
    band = jax.ShapeDtypeStruct((GROUPS * IMG_DEV, 128), f32)
    dma = pltpu.SemaphoreType.DMA
    out = pl.pallas_call(
        kernel,
        out_shape=(band, band, band, jax.ShapeDtypeStruct((1, PAIR_DEV), f32)),
        in_specs=[vmem] * 5 + [smem] * 5,
        out_specs=(vmem,) * 4,
        scratch_shapes=[
            pltpu.VMEM((PAIR_DEV * GROUPS * 2, 128), f32),
            pltpu.VMEM((PAIR_DEV * GROUPS, 128), f32),
            pltpu.VMEM((PAIR_DEV * GROUPS, 128), f32),
            pltpu.VMEM((PAIR_DEV, CODE_ROWS, 128), jnp.int16),
            pltpu.VMEM((OWNERS, MOST, CODE_ROWS, 128), jnp.int16),
            pltpu.VMEM((OWNERS, MOST, CODE_ROWS, 128), jnp.int16),
            pltpu.VMEM((OWNERS, 8, 128), jnp.int32),
            pltpu.VMEM((SLOTS, GROUPS, 128), f32),
            pltpu.VMEM((IMG_DEV, GROUPS, 128), f32),
            pltpu.VMEM((IMG_DEV, GROUPS, 128), f32),
            pltpu.VMEM((3, 8, 128), f32),
            pltpu.VMEM((IMG_DEV, VIEWS, 128), f32),
            pltpu.VMEM((VIEWS, 128), f32),
            pltpu.VMEM((IMG_DEV, VIEWS, 128), f32),
            pltpu.VMEM((VIEWS, 128), f32),
            pltpu.VMEM((ITERS, IMGS, 8, 128), f32),
            pltpu.VMEM((ITERS, OWNERS, 8, 128), f32),
            pltpu.SMEM((VIEWS,), jnp.int32),
            dma((OWNERS,)),
            dma((OWNERS,)),
            dma((OWNERS,)),
            dma((OWNERS,)),
            dma((ITERS, IMGS)),
            dma((ITERS, IMGS)),
            dma((ITERS, OWNERS)),
            dma((ITERS, OWNERS)),
        ],
        compiler_params=pltpu.CompilerParams(
            collective_id=0, has_side_effects=True, vmem_limit_bytes=48 * 2**20
        ),
        name="align",
    )(
        fold(log_depth),
        fold(moment_one),
        fold(moment_two),
        points,
        conf,
        image_pose,
        pair_pose,
        first_local,
        second_owner.reshape(PAIR_DEV),
        second_local,
    )
    return (unfold(out[0]), unfold(out[1]), unfold(out[2]), out[3].reshape(PAIR_DEV))


def solution(mesh):
    return jax.shard_map(
        shards,
        mesh=mesh,
        in_specs=(
            P("pair", "img"),
            P("pair", "img"),
            P("pair", "img"),
            P(),
            P("pair", None, "img"),
            P("pair", None, "img"),
            P(None, "pair"),
            P("pair"),
            P("pair", None),
            P("pair"),
        ),
        out_specs=(P("pair", "img"), P("pair", "img"), P("pair", "img"), P("pair")),
        check_vma=False,
    )
```

time: 658 us -> 120 us (0.18)
  waiting for transfers between devices: 482 us -> 0 us
  Pallas kernels: 0 us -> 107 us
  matrix products: 45.5 us -> 0 us
  other arithmetic: 43.1 us -> 0 us
  blocking collectives: 38.4 us -> 0 us
  local copies, waits for them, and re-layouts: 32.5 us -> 11.9 us
  between operations: 15.4 us -> 0.66 us
    unnamed x9 -> x0, waiting for transfers between devices: 360 us -> none
    all_gather x3 -> x0, waiting for transfers between devices: 122 us -> none  [shards(): block_rows = lax.all_gather(shared, 'pair', axis=0, tiled=True)]
    pallas_call x0 -> x1, Pallas kernels: none -> 107 us  [shards(): pl.pallas_call(kernel, out_shape=(band, band, band, jax.ShapeDtypeStruct(...]
    dot_general x14 -> x0, matrix products: 45.5 us -> none  [the longest x3 13.3 us: shards(): jnp.dot(image_chosen, second_terms, precision=highest)]
    psum x3 -> x0, blocking collectives: 38.4 us -> none  [pixel_sums(): return lax.psum(values, 'img')]
    unnamed x142 -> x24, local copies, waits for them, and re-layouts: 30.6 us -> 11.9 us
    another operation x12 -> x0, other arithmetic: 15.9 us -> none  [the longest x6 10.6 us: shards(): jnp.stack([jnp.stack(lever_one, axis=1), jnp.stack(lever_two, axis=1)], a...]
    reduce_sum x9 -> x0, other arithmetic: 14.3 us -> none  [the longest x3 8.99 us: shards(): gradient_pairs = 2.0 * weights * jnp.sum(residual * levers, axis=2)]
  transfers between devices with their start and end apart: 6 -> 0, of which waited for: 6 -> 0; matrix products, arithmetic and copies ran while one was open for 4% -> 0% of each run, Pallas kernels for 0% -> 0%
where the time goes in v1:
time: 120 us
  Pallas kernels  107 us (89%)
  local copies, waits for them, and re-layouts  11.9 us (10%)
    pallas_call x1, Pallas kernels, shards(): pl.pallas_call(kernel, out_shape=(band, band, band, jax.ShapeDtypeStruct(...  107 us
    unnamed x24, local copies, waits for them, and re-layouts  11.9 us

profile of v1, /device:TPU:1, one launch (start us, length us, event | category | flops | bytes accessed | tf_op | source)
XLA Modules:
  0.0 119.8 jit_solution(7484102020009858062)
XLA Ops:
  0.6 0.0 copy-start
  0.6 1.7 %copy-done = bf16[8,6,24576]{2,0,1:T(8,128)(2,1)S(1)} copy-done((bf16[8,6,24576]{2,0,1:T(8,128)(2,1)S(1)}, bf16[8,6,24576]{2,0,1:T(8,128)(2,1)}, u32[]{:S(2)}) %copy-start) | copy-done | bytes 2359320
  2.3 0.0 copy-start.1
  2.3 1.1 copy-done.1
  3.4 1.0 copy-done.2
  4.4 0.0 copy-start.3
  4.4 1.0 copy-done.3
  5.4 0.0 copy-start.4
  5.4 1.0 copy-done.4
  6.4 0.0 copy-start.5
  6.4 0.7 copy-done.5
  7.1 0.0 copy-start.6
  7.1 0.7 copy-done.6
  7.8 0.0 copy-start.7
  7.8 0.7 copy-done.7
  8.5 0.0 copy-start.8
  8.5 0.7 copy-done.8
  9.1 0.0 copy-start.9
  9.1 0.7 copy-done.9
  9.8 107.3 %align.1 = (f32[768,128]{1,0:T(8,128)S(1)}, f32[768,128]{1,0:T(8,128)S(1)}, f32[768,128]{1,0:T(8,128)S(1)}, f32[1,8]{1,0:T(1,128)S(1)}) custom-call(f32[768,128]{1,0:T(8,128)S(1)} %bitcast.40, f32[768,128]{1,0:T(8,128)S(1)} %bitcast.41, f32[768,128]{1,0:T(8,128)S(1)} %bitcast.42, bf16[6,8,24576]{2,1,0:T(8,128)(2,1)S(1)} %bitcast.38, ...), custom_call_target="tpu_custom_call" | custom-call | tf_op jit(solution)/shard_map/align/pallas_call | solution.py:581
  117.1 0.7 copy.25
  117.8 0.7 copy.26
  118.6 0.7 copy.27
  119.3 0.5 copy.28
  (1 shorter events, 0.0 us)
Async XLA Ops:
  0.6 1.7 %copy-start = (bf16[8,6,24576]{2,0,1:T(8,128)(2,1)S(1)}, bf16[8,6,24576]{2,0,1:T(8,128)(2,1)}, u32[]{:S(2)}) copy-start(bf16[8,6,24576]{2,0,1:T(8,128)(2,1)} %param.14) | copy-start | bytes 7077892
  2.3 1.1 copy-start.1
  3.4 1.0 copy-start.2
  4.4 1.0 copy-start.3
  5.4 1.0 copy-start.4
  6.4 0.7 copy-start.5
  7.1 0.7 copy-start.6
  7.8 0.7 copy-start.7
  8.5 0.7 copy-start.8
  9.1 0.7 copy-start.9

commit v2 on v1

--- a/solution.py
+++ b/solution.py
@@ -14,8 +14,10 @@
 MOST = 2
 IMGS = 8
 OWNERS = 16
+XS = 4
 YS = 4
 ZS = 4
+CHIPS = XS * YS * ZS
 BAND = ROWS * COLS // IMGS
 GROUPS = BAND // 128
 BLOCKS = GROUPS // 8
@@ -23,7 +25,9 @@
 SLOTS = OWNERS * MOST
 VIEWS = PAIR_DEV + SLOTS
 CODE_ROWS = 2 * GROUPS + 16
-TILE = 4
+TILE = 12
+PART = 4
+UNROLL = 4
 LEVELS = 32700.0
 SCALE_STEPS = 64.0
 
@@ -61,6 +65,21 @@
 
 
 def kernel(
+    log_hbm,
+    one_hbm,
+    two_hbm,
+    points_hbm,
+    conf_hbm,
+    image_pose_hbm,
+    pair_pose_hbm,
+    first_local_hbm,
+    second_owner_hbm,
+    second_local_hbm,
+    log_out,
+    one_out,
+    two_out,
+    scale_out,
+    scale_ref,
     log_ref,
     one_ref,
     two_ref,
@@ -71,10 +90,6 @@
     first_local,
     second_owner,
     second_local,
-    log_out,
-    one_out,
-    two_out,
-    scale_out,
     conf_f,
     stage_one,
     stage_two,
@@ -83,6 +98,7 @@
     recv_buf,
     meta,
     cu_ref,
+    prefix_ref,
     weight_sum,
     depth_ref,
     tau_ref,
@@ -90,18 +106,40 @@
     mask_ref,
     weight_ref,
     inner_ref,
-    img_buf,
-    pair_buf,
-    image_tab,
+    core_buf,
+    chip_buf,
+    table_ref,
+    table,
+    load_sem,
+    store_sem,
+    table_sem,
     send_sem,
     recv_sem,
     meta_send,
     meta_recv,
-    img_send,
-    img_recv,
-    pair_send,
-    pair_recv,
+    core_send,
+    core_recv,
+    chip_send,
+    chip_recv,
 ):
+    def load(n, src, dst):
+        copy = pltpu.make_async_copy(src, dst, load_sem.at[n])
+        copy.start()
+        return copy
+
+    small = [
+        load(0, second_owner_hbm, second_owner),
+        load(1, second_local_hbm, second_local),
+        load(2, first_local_hbm, first_local),
+        load(3, pair_pose_hbm, pair_pose),
+        load(4, image_pose_hbm, image_pose),
+    ]
+    conf_load = load(5, conf_hbm, conf_ref)
+    second_load = load(6, points_hbm.at[pl.ds(3, 3)], points_ref.at[pl.ds(3, 3)])
+    first_load = load(7, points_hbm.at[pl.ds(0, 3)], points_ref.at[pl.ds(0, 3)])
+    log_load = load(8, log_hbm, log_ref)
+    state_loads = [load(9, one_hbm, one_ref), load(10, two_hbm, two_ref)]
+
     my_img = lax.axis_index("img")
     my_pair = lax.axis_index("pair")
     my_y = my_pair // ZS
@@ -112,19 +150,30 @@
 
     barrier = pltpu.get_barrier_semaphore()
 
-    def greet_pair(k, carry):
-        pl.semaphore_signal(barrier, 1, device_id=(my_img, pair_at(k, -1)), device_id_type=MESH)
-        return carry
-
-    def greet_img(k, carry):
-        pl.semaphore_signal(barrier, 1, device_id=((my_img + k) % IMGS, my_pair), device_id_type=MESH)
-        return carry
-
-    lax.fori_loop(1, OWNERS, greet_pair, 0)
-    lax.fori_loop(1, IMGS, greet_img, 0)
+    my_x = my_img // 2
+    my_core = my_img % 2
+    my_chip = my_x * OWNERS + my_pair
+    xs = [(my_x + d) % XS for d in range(XS)]
+    ys = [(my_y + d) % YS for d in range(YS)]
+    zs = [(my_z + d) % ZS for d in range(ZS)]
+    offsets = [(a, b, c) for a in range(XS) for b in range(YS) for c in range(ZS) if (a, b, c) != (0, 0, 0)]
+    offsets.sort(key=lambda o: -sum(min(d, 4 - d) for d in o))
+
+    def greet_chip(k, carry):
+        x = (my_x + k // OWNERS) % XS
+        y = (my_y + k // ZS) % YS
+        z = (my_z + k) % ZS
+        pl.semaphore_signal(barrier, 1, device_id=(x * 2 + my_core, y * ZS + z), device_id_type=MESH)
+        return carry
+
+    pl.semaphore_signal(barrier, 1, device_id=(my_img + 1 - 2 * my_core, my_pair), device_id_type=MESH)
+    lax.fori_loop(1, CHIPS, greet_chip, 0)
 
     sub = lax.broadcasted_iota(jnp.int32, (8, 128), 0)
     lane = lax.broadcasted_iota(jnp.int32, (8, 128), 1)
+
+    for copy in small:
+        copy.wait()
 
     owners = [second_owner[e] for e in range(PAIR_DEV)]
     order = []
@@ -162,7 +211,9 @@
         conf_f[rows, :] = conf_ref[rows, :].astype(f32)
         return carry
 
+    conf_load.wait()
     lax.fori_loop(0, PAIR_DEV * 2 * GROUPS // 64, widen, 0)
+    second_load.wait()
 
     def prepare(view, images, stage, scaled):
         cols = [column([image_pose[i, images[e]] for e in range(PAIR_DEV)]) for i in range(7)]
@@ -231,7 +282,7 @@
     for j in range(MOST):
         recv_buf[0, j] = codes[slot_pair(0, j)]
 
-    pl.semaphore_wait(barrier, OWNERS - 1 + IMGS - 1)
+    pl.semaphore_wait(barrier, CHIPS)
 
     def meta_copy(k):
         return pltpu.make_async_remote_copy(
@@ -266,6 +317,7 @@
     lax.fori_loop(1, OWNERS, start_meta, 0)
     lax.fori_loop(1, OWNERS, start_slots, 0)
 
+    first_load.wait()
     square_one, dot_one = prepare(0, firsts, stage_one, True)
 
     def depth_of(values):
@@ -282,7 +334,10 @@
             depth_ref[v, block_rows(block), :] = depth_of(log_ref[image_rows(block, v), :])
         return carry
 
+    log_load.wait()
     lax.fori_loop(0, BLOCKS, first_depth, 0)
+    for copy in state_loads:
+        copy.wait()
 
     own = [[image_pose[i, my_pair * IMG_DEV + min(v, IMG_DEV - 1)] for v in range(8)] for i in range(7)]
     own_cols = [column(own[i]) for i in range(7)]
@@ -314,35 +369,54 @@
         for v in range(IMG_DEV):
             found = jnp.where(held & (local_row == v), 1.0, 0.0)
             hot_ref[v, rows, :] = jnp.broadcast_to(jnp.sum(found, axis=1, keepdims=True), (8, 128))
-    for e in range(PAIR_DEV):
-        image_tab[e] = first_local[e]
-
-    def find_image(r, carry):
-        image_tab[PAIR_DEV + r] = jnp.sum(jnp.where((slot_of == r) & (sub == 0), local_row, 0))
-        return carry
-
-    lax.fori_loop(0, SLOTS, find_image, 0)
-
-    def first_cu(e, block):
-        return stage_one[pl.ds(block * 64 + e, 8, stride=8), :]
-
-    def dot_first(e, carry):
-        v = image_tab[e]
-        total = jnp.zeros((8, 128), f32)
+
+    image_row = jnp.zeros((8, 128), jnp.int32)
+    for group in range(VIEWS // 8):
+        if group == 0:
+            image_col = local_first
+        else:
+            held = (slot_of == sub + (group - 1) * 8).astype(jnp.int32)
+            image_col = jnp.sum(held * (local_row - IMG_DEV), axis=1, keepdims=True) + IMG_DEV
+        found = jnp.where(lane == sub + group * 8, image_col, 0)
+        image_row = image_row + jnp.broadcast_to(jnp.sum(found, axis=0, keepdims=True), (8, 128))
+    order_row = jnp.zeros((8, 128), jnp.int32)
+    listed = lane < VIEWS
+    for group in range(VIEWS // 8):
+        view = sub + group * 8
+        found = jnp.where(lane == view, image_row, 0)
+        image_col = jnp.sum(found, axis=1, keepdims=True)
+        before = listed & ((image_row < image_col) | ((image_row == image_col) & (lane < view)))
+        place = jnp.sum(before.astype(jnp.int32), axis=1, keepdims=True)
+        found = jnp.where(lane == place, view, 0)
+        order_row = order_row + jnp.broadcast_to(jnp.sum(found, axis=0, keepdims=True), (8, 128))
+    end_row = jnp.zeros((8, 128), jnp.int32)
+    for v in range(IMG_DEV):
+        upto = (listed & (image_row <= v)).astype(jnp.int32)
+        end_row = jnp.where(lane == v, jnp.sum(upto, axis=1, keepdims=True), end_row)
+    image_row = jnp.minimum(image_row, IMG_DEV - 1)
+    table_ref[...] = jnp.where(sub == 0, image_row, jnp.where(sub == 1, order_row, end_row))
+    table_copy = pltpu.make_async_copy(table_ref, table, table_sem)
+    table_copy.start()
+
+    def first_copy(e, carry):
         for block in range(BLOCKS):
-            total = total + first_cu(e, block) * depth_ref[v, block * 8 : block * 8 + 8, :]
-        inner_ref[pl.ds(e, 1), :] = jnp.sum(total, axis=0, keepdims=True)
-        return carry
-
-    def dot_second(r, carry):
-        v = image_tab[PAIR_DEV + r]
-        total = jnp.zeros((8, 128), f32)
+            cu_ref[e, block * 8 : block * 8 + 8, :] = stage_one[pl.ds(block * 64 + e, 8, stride=8), :]
+        return carry
+
+    lax.fori_loop(0, PAIR_DEV, first_copy, 0)
+    table_copy.wait()
+
+    def dot_view(r, carry):
+        v = table[0, r]
+        totals = [jnp.zeros((8, 128), f32) for n in range(PART)]
         for block in range(BLOCKS):
-            total = total + cu_ref[r, block * 8 : block * 8 + 8, :] * depth_ref[v, block * 8 : block * 8 + 8, :]
-        inner_ref[pl.ds(PAIR_DEV + r, 1), :] = jnp.sum(total, axis=0, keepdims=True)
-        return carry
-
-    lax.fori_loop(0, PAIR_DEV, dot_first, 0)
+            rows = slice(block * 8, block * 8 + 8)
+            totals[block % PART] = totals[block % PART] + cu_ref[r, rows, :] * depth_ref[v, rows, :]
+        total = (totals[0] + totals[1]) + (totals[2] + totals[3])
+        inner_ref[pl.ds(r, 1), :] = jnp.sum(total, axis=0, keepdims=True)
+        return carry
+
+    lax.fori_loop(0, PAIR_DEV, dot_view, 0)
 
     def first_sums(block, carry):
         sums = [jnp.zeros((8, 128), f32) for v in range(IMG_DEV)]
@@ -368,7 +442,7 @@
             units.append(unit)
             slot = PAIR_DEV + k * MOST + j
             hots.append([hot_ref[v, pl.ds(slot, 1), :] * (1.0 / 128.0) for v in range(IMG_DEV)])
-            images.append(image_tab[slot])
+            images.append(table[0, slot])
 
         def part(half, totals):
             totals = list(totals)
@@ -379,7 +453,7 @@
                 value = recv_buf[k, j, rows, :].astype(jnp.int32).astype(f32)
                 weight = recv_buf[k, j, weight_rows, :].astype(jnp.int32).astype(f32)
                 cu = value * units[j] * weight
-                cu_ref[k * MOST + j, rows, :] = cu
+                cu_ref[PAIR_DEV + k * MOST + j, rows, :] = cu
                 totals[j] = totals[j] + cu * depth_ref[images[j], rows, :]
                 for v in range(IMG_DEV):
                     sums[v] = sums[v] + weight * hots[j][v]
@@ -400,67 +474,52 @@
     fixed_row = pair_row(dot_one + dot_two)
     square_row = pair_row(square_one + square_two)
 
-    def img_copy(t, k):
+    def core_copy(t):
         return pltpu.make_async_remote_copy(
-            src_ref=img_buf.at[t, my_img],
-            dst_ref=img_buf.at[t, my_img],
-            send_sem=img_send.at[t, k],
-            recv_sem=img_recv.at[t, my_img],
-            device_id=((my_img + k) % IMGS, my_pair),
+            src_ref=core_buf.at[t, 0],
+            dst_ref=core_buf.at[t, 1],
+            send_sem=core_send.at[t],
+            recv_sem=core_recv.at[t],
+            device_id=(my_img + 1 - 2 * my_core, my_pair),
             device_id_type=MESH,
         )
 
-    def img_arrival(t, k):
-        source = (my_img + k) % IMGS
+    def chip_copy(t, n, arrival):
+        a, b, c = offsets[n]
+        pair = ys[b] * ZS + zs[c]
+        place = xs[a] * OWNERS + pair if arrival else my_chip
         return pltpu.make_async_remote_copy(
-            src_ref=img_buf.at[t, source],
-            dst_ref=img_buf.at[t, source],
-            send_sem=img_send.at[t, k],
-            recv_sem=img_recv.at[t, source],
-            device_id=(source, my_pair),
+            src_ref=chip_buf.at[t, place],
+            dst_ref=chip_buf.at[t, place],
+            send_sem=chip_send.at[t, n],
+            recv_sem=chip_recv.at[t, place],
+            device_id=(xs[a] * 2 + my_core, pair),
             device_id_type=MESH,
         )
 
-    def pair_copy(t, k):
-        return pltpu.make_async_remote_copy(
-            src_ref=pair_buf.at[t, my_pair],
-            dst_ref=pair_buf.at[t, my_pair],
-            send_sem=pair_send.at[t, k],
-            recv_sem=pair_recv.at[t, my_pair],
-            device_id=(my_img, pair_at(k, 1)),
-            device_id_type=MESH,
-        )
-
-    def pair_arrival(t, k):
-        source = pair_at(k, 1)
-        return pltpu.make_async_remote_copy(
-            src_ref=pair_buf.at[t, source],
-            dst_ref=pair_buf.at[t, source],
-            send_sem=pair_send.at[t, k],
-            recv_sem=pair_recv.at[t, source],
-            device_id=(my_img, source),
-            device_id_type=MESH,
-        )
-
     def sum_all(t, tile):
-        img_buf[t, my_img] = tile
-        for k in range(1, IMGS):
-            img_copy(t, k).start()
-        for k in range(1, IMGS):
-            img_arrival(t, k).wait_recv()
-        total = img_buf[t, 0]
-        for k in range(1, IMGS):
-            total = total + img_buf[t, k]
-        pair_buf[t, my_pair] = total
-        for k in range(1, OWNERS):
-            pair_copy(t, k).start()
-        for k in range(1, OWNERS):
-            pair_arrival(t, k).wait_recv()
-        total = pair_buf[t, 0]
-        for k in range(1, OWNERS):
-            total = total + pair_buf[t, k]
-        return total
-
+        core_buf[t, 0] = tile
+        core_copy(t).start()
+        core_copy(t).wait_recv()
+        chip_buf[t, my_chip] = tile + core_buf[t, 1]
+        for n in range(CHIPS - 1):
+            chip_copy(t, n, False).start()
+        for n in reversed(range(CHIPS - 1)):
+            chip_copy(t, n, True).wait_recv()
+        parts = [chip_buf[t, n] for n in range(CHIPS)]
+        while len(parts) > 1:
+            parts = [parts[n] + parts[n + 1] for n in range(0, len(parts), 2)]
+        return parts[0]
+
+    def stores(tile_id):
+        rows = pl.ds(pl.multiple_of(tile_id * TILE * 32, 8), TILE * 32)
+        pairs = [(log_ref, log_out), (one_ref, one_out), (two_ref, two_out)]
+        return [
+            pltpu.make_async_copy(a.at[rows], b.at[rows], store_sem.at[tile_id, n])
+            for n, (a, b) in enumerate(pairs)
+        ]
+
+    scale_store = pltpu.make_async_copy(scale_ref, scale_out, load_sem.at[0])
     denominator = None
     for sweep in range(ITERS):
         row = jnp.zeros((8, 128), f32)
@@ -468,8 +527,8 @@
             rows = slice(group * 8, group * 8 + 8)
             row = row + jnp.sum(inner_ref[rows, :], axis=1, keepdims=True) * mask_ref[rows, :]
         row = jnp.sum(row, axis=0, keepdims=True) + fixed_row
-        tile = jnp.where(sub == 0, row, jnp.where(sub == 1, square_row, 0.0))
-        total = sum_all(sweep, tile)
+        two = lax.broadcasted_iota(jnp.int32, (2, 128), 0)
+        total = sum_all(sweep, jnp.where(two == 0, row, square_row))
         if sweep == 0:
             denominator = total[1:2]
         scales = jnp.broadcast_to(total[0:1] / denominator, (8, 128))
@@ -478,9 +537,9 @@
             held = jnp.sum(scales * mask_ref[rows, :], axis=1, keepdims=True)
             if group == 0 and sweep == ITERS - 1:
                 own_row = jnp.sum(jnp.where(lane == sub, held, 0.0), axis=0, keepdims=True)
-                scale_out[...] = own_row[:, 0:PAIR_DEV]
-            for v in range(IMG_DEV):
-                weight_ref[v, rows, :] = held * hot_ref[v, rows, :]
+                scale_ref[...] = own_row[:, 0:PAIR_DEV]
+                scale_store.start()
+            weight_ref[rows, :] = jnp.broadcast_to(held, (8, 128))
 
         steps = START + sweep + 1
         bias_one = 1 - beta_one**steps
@@ -490,27 +549,24 @@
         def update(tile_id, carry):
             start = tile_id * TILE
 
-            def gather_first(e, sums):
+            def gather(step, sums):
                 sums = list(sums)
-                for n in range(TILE):
-                    cu = first_cu(e, start + n)
-                    for v in range(IMG_DEV):
-                        sums[n * IMG_DEV + v] = sums[n * IMG_DEV + v] + cu * weight_ref[v, pl.ds(e, 1), :]
+                for n in range(UNROLL):
+                    q = step * UNROLL + n
+                    r = table[1, q]
+                    weight = weight_ref[pl.ds(r, 1), :]
+                    for m in range(TILE):
+                        sums[m] = sums[m] + cu_ref[r, block_rows(start + m), :] * weight
+                        prefix_ref[q + 1, m * 8 : m * 8 + 8, :] = sums[m]
                 return tuple(sums)
 
-            def gather_second(r, sums):
-                sums = list(sums)
-                for n in range(TILE):
-                    cu = cu_ref[r, block_rows(start + n), :]
-                    for v in range(IMG_DEV):
-                        sums[n * IMG_DEV + v] = sums[n * IMG_DEV + v] + cu * weight_ref[v, pl.ds(PAIR_DEV + r, 1), :]
-                return tuple(sums)
-
-            sums = tuple(jnp.zeros((8, 128), f32) for i in range(TILE * IMG_DEV))
-            sums = lax.fori_loop(0, PAIR_DEV, gather_first, sums)
-            sums = lax.fori_loop(0, SLOTS, gather_second, sums)
-            for n in range(TILE):
+            zero = jnp.zeros((8, 128), f32)
+            for m in range(TILE):
+                prefix_ref[0, m * 8 : m * 8 + 8, :] = zero
+            lax.fori_loop(0, VIEWS // UNROLL, gather, (zero,) * TILE)
+            def step_adam(n, carry):
                 block = start + n
+                here = pl.ds(pl.multiple_of(n * 8, 8), 8)
                 down = (block * 2 + sub // 4).astype(f32) + first_row
                 rays_y = (down + 0.5 - ROWS / 2) / COLS
                 rays_x = (((sub % 4) * 128 + lane).astype(f32) + 0.5 - COLS / 2) / COLS
@@ -518,28 +574,41 @@
                 for v in range(IMG_DEV):
                     depth = depth_ref[v, block_rows(block), :]
                     lever = rays_x * tau_ref[0, v : v + 1, :] + rays_y * tau_ref[1, v : v + 1, :] + tau_ref[2, v : v + 1, :]
-                    pull = (depth * length + lever) * weight_sum[v, block_rows(block), :] - sums[n * IMG_DEV + v]
+                    gathered = prefix_ref[table[2, v], here, :]
+                    if v > 0:
+                        gathered = gathered - prefix_ref[table[2, v - 1], here, :]
+                    pull = (depth * length + lever) * weight_sum[v, block_rows(block), :] - gathered
                     gradient = 2.0 * depth * pull
                     rows = image_rows(block, v)
-                    old_one = (one_ref if sweep == 0 else one_out)[rows, :]
-                    old_two = (two_ref if sweep == 0 else two_out)[rows, :]
-                    old_log = (log_ref if sweep == 0 else log_out)[rows, :]
+                    old_one = one_ref[rows, :]
+                    old_two = two_ref[rows, :]
+                    old_log = log_ref[rows, :]
                     new_one = beta_one * old_one + (1 - beta_one) * gradient
                     new_two = beta_two * old_two + (1 - beta_two) * gradient * gradient
                     corrected_one = new_one * (1 / bias_one)
                     corrected_two = new_two * (1 / bias_two)
                     new_log = old_log - learn_rate * corrected_one / (jnp.sqrt(corrected_two) + adam_eps)
-                    one_out[rows, :] = new_one
-                    two_out[rows, :] = new_two
-                    log_out[rows, :] = new_log
+                    one_ref[rows, :] = new_one
+                    two_ref[rows, :] = new_two
+                    log_ref[rows, :] = new_log
                     if not last:
                         depth_ref[v, block_rows(block), :] = depth_of(new_log)
+                return carry
+
+            lax.fori_loop(0, TILE, step_adam, 0)
+            if last:
+                for copy in stores(tile_id):
+                    copy.start()
             return carry
 
         lax.fori_loop(0, BLOCKS // TILE, update, 0)
         if not last:
-            lax.fori_loop(0, PAIR_DEV, dot_first, 0)
-            lax.fori_loop(0, SLOTS, dot_second, 0)
+            lax.fori_loop(0, VIEWS, dot_view, 0)
+
+    scale_store.wait()
+    for tile_id in range(BLOCKS // TILE):
+        for copy in stores(tile_id):
+            copy.wait()
 
     def finish(k, carry):
         meta_copy(k).wait_send()
@@ -548,10 +617,22 @@
 
     lax.fori_loop(1, OWNERS, finish, 0)
     for t in range(ITERS):
-        for k in range(1, IMGS):
-            img_copy(t, k).wait_send()
-        for k in range(1, OWNERS):
-            pair_copy(t, k).wait_send()
+        core_copy(t).wait_send()
+        for n in range(CHIPS - 1):
+            chip_copy(t, n, False).wait_send()
+
+
+def store(log_ref, one_ref, two_ref, scale_ref, log_out, one_out, two_out, scale_out, sem):
+    copies = [
+        pltpu.make_async_copy(log_ref, log_out, sem.at[0]),
+        pltpu.make_async_copy(one_ref, one_out, sem.at[1]),
+        pltpu.make_async_copy(two_ref, two_out, sem.at[2]),
+        pltpu.make_async_copy(scale_ref, scale_out, sem.at[3]),
+    ]
+    for copy in copies:
+        copy.start()
+    for copy in copies:
+        copy.wait()
 
 
 def shards(
@@ -574,16 +655,26 @@
 
     points = pair_points.transpose(1, 0, 2)
     conf = confidence.reshape(PAIR_DEV, 2, GROUPS, 128).transpose(0, 2, 1, 3).reshape(PAIR_DEV * GROUPS * 2, 128)
-    vmem = pl.BlockSpec(memory_space=pltpu.VMEM)
-    smem = pl.BlockSpec(memory_space=pltpu.SMEM)
+    hbm = pl.BlockSpec(memory_space=pltpu.HBM)
     band = jax.ShapeDtypeStruct((GROUPS * IMG_DEV, 128), f32)
     dma = pltpu.SemaphoreType.DMA
     out = pl.pallas_call(
         kernel,
         out_shape=(band, band, band, jax.ShapeDtypeStruct((1, PAIR_DEV), f32)),
-        in_specs=[vmem] * 5 + [smem] * 5,
-        out_specs=(vmem,) * 4,
+        in_specs=[hbm] * 10,
+        out_specs=(hbm,) * 4,
         scratch_shapes=[
+            pltpu.VMEM((1, PAIR_DEV), f32),
+            pltpu.VMEM((GROUPS * IMG_DEV, 128), f32),
+            pltpu.VMEM((GROUPS * IMG_DEV, 128), f32),
+            pltpu.VMEM((GROUPS * IMG_DEV, 128), f32),
+            pltpu.VMEM((6, PAIR_DEV, BAND), jnp.bfloat16),
+            pltpu.VMEM((PAIR_DEV * GROUPS * 2, 128), jnp.bfloat16),
+            pltpu.SMEM((7, IMG_DEV * OWNERS), f32),
+            pltpu.SMEM((7, PAIR_DEV), f32),
+            pltpu.SMEM((PAIR_DEV,), jnp.int32),
+            pltpu.SMEM((PAIR_DEV,), jnp.int32),
+            pltpu.SMEM((PAIR_DEV,), jnp.int32),
             pltpu.VMEM((PAIR_DEV * GROUPS * 2, 128), f32),
             pltpu.VMEM((PAIR_DEV * GROUPS, 128), f32),
             pltpu.VMEM((PAIR_DEV * GROUPS, 128), f32),
@@ -591,28 +682,33 @@
             pltpu.VMEM((OWNERS, MOST, CODE_ROWS, 128), jnp.int16),
             pltpu.VMEM((OWNERS, MOST, CODE_ROWS, 128), jnp.int16),
             pltpu.VMEM((OWNERS, 8, 128), jnp.int32),
-            pltpu.VMEM((SLOTS, GROUPS, 128), f32),
+            pltpu.VMEM((VIEWS, GROUPS, 128), f32),
+            pltpu.VMEM((VIEWS + 1, TILE * 8, 128), f32),
             pltpu.VMEM((IMG_DEV, GROUPS, 128), f32),
             pltpu.VMEM((IMG_DEV, GROUPS, 128), f32),
             pltpu.VMEM((3, 8, 128), f32),
             pltpu.VMEM((IMG_DEV, VIEWS, 128), f32),
             pltpu.VMEM((VIEWS, 128), f32),
-            pltpu.VMEM((IMG_DEV, VIEWS, 128), f32),
             pltpu.VMEM((VIEWS, 128), f32),
-            pltpu.VMEM((ITERS, IMGS, 8, 128), f32),
-            pltpu.VMEM((ITERS, OWNERS, 8, 128), f32),
-            pltpu.SMEM((VIEWS,), jnp.int32),
+            pltpu.VMEM((VIEWS, 128), f32),
+            pltpu.VMEM((ITERS, 2, 2, 128), f32),
+            pltpu.VMEM((ITERS, CHIPS, 2, 128), f32),
+            pltpu.VMEM((8, 128), jnp.int32),
+            pltpu.SMEM((8, 128), jnp.int32),
+            dma((11,)),
+            dma((BLOCKS // TILE, 3)),
+            dma,
             dma((OWNERS,)),
             dma((OWNERS,)),
             dma((OWNERS,)),
             dma((OWNERS,)),
-            dma((ITERS, IMGS)),
-            dma((ITERS, IMGS)),
-            dma((ITERS, OWNERS)),
-            dma((ITERS, OWNERS)),
+            dma((ITERS,)),
+            dma((ITERS,)),
+            dma((ITERS, CHIPS)),
+            dma((ITERS, CHIPS)),
         ],
         compiler_params=pltpu.CompilerParams(
-            collective_id=0, has_side_effects=True, vmem_limit_bytes=48 * 2**20
+            collective_id=0, has_side_effects=True, vmem_limit_bytes=60 * 2**20
         ),
         name="align",
     )(
@@ -627,6 +723,15 @@
         second_owner.reshape(PAIR_DEV),
         second_local,
     )
+    out = pl.pallas_call(
+        store,
+        out_shape=(band, band, band, jax.ShapeDtypeStruct((1, PAIR_DEV), f32)),
+        in_specs=[hbm] * 4,
+        out_specs=(hbm,) * 4,
+        scratch_shapes=[dma((4,))],
+        compiler_params=pltpu.CompilerParams(vmem_limit_bytes=60 * 2**20),
+        name="store",
+    )(*out)
     return (unfold(out[0]), unfold(out[1]), unfold(out[2]), out[3].reshape(PAIR_DEV))
 
 

time: 120 us -> 137 us (1.14)
  Pallas kernels: 107 us -> 136 us
  local copies, waits for them, and re-layouts: 11.9 us -> 0 us
    pallas_call x0 -> x1, Pallas kernels: none -> 36.9 us  [shards(): pl.pallas_call(store, out_shape=(band, band, band, jax.ShapeDtypeStruct((...]
    unnamed x24 -> x0, local copies, waits for them, and re-layouts: 11.9 us -> none
    pallas_call x1, Pallas kernels: 107 us -> 98.9 us  [shards(): pl.pallas_call(kernel, out_shape=(band, band, band, jax.ShapeDtypeStruct(...]
where the time goes in v2:
time: 137 us; the launch traced here: 136 us
  Pallas kernels  136 us (99%)
    pallas_call x1, Pallas kernels, shards(): pl.pallas_call(kernel, out_shape=(band, band, band, jax.ShapeDtypeStruct(...  98.9 us
    pallas_call x1, Pallas kernels, shards(): pl.pallas_call(store, out_shape=(band, band, band, jax.ShapeDtypeStruct((...  36.9 us

profile of v2, /device:TPU:1, one launch (start us, length us, event | category | flops | bytes accessed | tf_op | source)
XLA Modules:
  0.0 136.4 jit_solution(16841160594291391037)
XLA Ops:
  0.6 98.9 %align.1 = (f32[768,128]{1,0:T(8,128)}, f32[768,128]{1,0:T(8,128)}, f32[768,128]{1,0:T(8,128)}, f32[1,8]{1,0:T(1,128)}) custom-call(f32[768,128]{1,0:T(8,128)} %bitcast.40, f32[768,128]{1,0:T(8,128)} %bitcast.41, f32[768,128]{1,0:T(8,128)} %bitcast.42, bf16[6,8,24576]{2,1,0:T(8,128)(2,1)} %bitcast.38, bf16[3072,128]{1,0:T(8,128)(2,1)} %bitcast.39, ...), custom_call_target="tpu_custom_call" | custom-call | tf_op jit(solution)/shard_map/align/pallas_call | solution.py:661
  99.5 36.9 %store.1 = (f32[768,128]{1,0:T(8,128)}, f32[768,128]{1,0:T(8,128)}, f32[768,128]{1,0:T(8,128)}, f32[1,8]{1,0:T(1,128)}) custom-call(f32[768,128]{1,0:T(8,128)} %get-tuple-element.12.log_ref, f32[768,128]{1,0:T(8,128)} %get-tuple-element.13.one_ref, f32[768,128]{1,0:T(8,128)} %get-tuple-element.14.two_ref, f32[1,8]{1,0:T(1,128)} %get-tuple-element.15.scale_ref), custom_call_target="tpu_custom_call" | custom-call | tf_op jit(solution)/shard_map/store/pallas_call | solution.py:726

commit v3 on v2

--- a/solution.py
+++ b/solution.py
@@ -622,16 +622,21 @@
             chip_copy(t, n, False).wait_send()
 
 
-def store(log_ref, one_ref, two_ref, scale_ref, log_out, one_out, two_out, scale_out, sem):
-    copies = [
-        pltpu.make_async_copy(log_ref, log_out, sem.at[0]),
-        pltpu.make_async_copy(one_ref, one_out, sem.at[1]),
-        pltpu.make_async_copy(two_ref, two_out, sem.at[2]),
-        pltpu.make_async_copy(scale_ref, scale_out, sem.at[3]),
-    ]
-    for copy in copies:
+def store(log_in, one_in, two_in, scale_in, log_out, one_out, two_out, scale_out, bands, scale, in_sem, out_sem):
+    half = GROUPS * IMG_DEV // 2
+    moves = [(scale_in, scale, scale_out)]
+    for part in range(2):
+        rows = pl.ds(part * half, half)
+        for n, (a, b) in enumerate([(log_in, log_out), (one_in, one_out), (two_in, two_out)]):
+            moves.append((a.at[rows], bands.at[n, rows], b.at[rows]))
+    loads = [pltpu.make_async_copy(a, m, in_sem.at[n]) for n, (a, m, b) in enumerate(moves)]
+    stores = [pltpu.make_async_copy(m, b, out_sem.at[n]) for n, (a, m, b) in enumerate(moves)]
+    for copy in loads:
         copy.start()
-    for copy in copies:
+    for arrived, copy in zip(loads, stores):
+        arrived.wait()
+        copy.start()
+    for copy in stores:
         copy.wait()
 
 
@@ -728,7 +733,12 @@
         out_shape=(band, band, band, jax.ShapeDtypeStruct((1, PAIR_DEV), f32)),
         in_specs=[hbm] * 4,
         out_specs=(hbm,) * 4,
-        scratch_shapes=[dma((4,))],
+        scratch_shapes=[
+            pltpu.VMEM((3, GROUPS * IMG_DEV, 128), f32),
+            pltpu.VMEM((1, PAIR_DEV), f32),
+            dma((7,)),
+            dma((7,)),
+        ],
         compiler_params=pltpu.CompilerParams(vmem_limit_bytes=60 * 2**20),
         name="store",
     )(*out)

time: 137 us -> 102 us (0.74)
  Pallas kernels: 136 us -> 101 us
    pallas_call x1, Pallas kernels: 36.9 us -> 2.15 us  [shards(): pl.pallas_call(store, out_shape=(band, band, band, jax.ShapeDtypeStruct((...]
where the time goes in v3:
time: 102 us
  Pallas kernels  101 us (99%)
    pallas_call x1, Pallas kernels, shards(): pl.pallas_call(kernel, out_shape=(band, band, band, jax.ShapeDtypeStruct(...  98.9 us
    pallas_call x1, Pallas kernels, shards(): pl.pallas_call(store, out_shape=(band, band, band, jax.ShapeDtypeStruct((...  2.15 us

profile of v3, /device:TPU:1, one launch (start us, length us, event | category | flops | bytes accessed | tf_op | source)
XLA Modules:
  0.0 101.7 jit_solution(13935290880433418491)
XLA Ops:
  0.6 98.9 %align.1 = (f32[768,128]{1,0:T(8,128)}, f32[768,128]{1,0:T(8,128)}, f32[768,128]{1,0:T(8,128)}, f32[1,8]{1,0:T(1,128)}) custom-call(f32[768,128]{1,0:T(8,128)} %bitcast.40, f32[768,128]{1,0:T(8,128)} %bitcast.41, f32[768,128]{1,0:T(8,128)} %bitcast.42, bf16[6,8,24576]{2,1,0:T(8,128)(2,1)} %bitcast.38, bf16[3072,128]{1,0:T(8,128)(2,1)} %bitcast.39, ...), custom_call_target="tpu_custom_call" | custom-call | tf_op jit(solution)/shard_map/align/pallas_call | solution.py:666
  99.5 2.2 %store.1 = (f32[768,128]{1,0:T(8,128)}, f32[768,128]{1,0:T(8,128)}, f32[768,128]{1,0:T(8,128)}, f32[1,8]{1,0:T(1,128)}) custom-call(f32[768,128]{1,0:T(8,128)} %get-tuple-element.12.log_in, f32[768,128]{1,0:T(8,128)} %get-tuple-element.13.one_in, f32[768,128]{1,0:T(8,128)} %get-tuple-element.14.two_in, f32[1,8]{1,0:T(1,128)} %get-tuple-element.15.scale_in), custom_call_target="tpu_custom_call" | custom-call | tf_op jit(solution)/shard_map/store/pallas_call | solution.py:731

commit v4 on v3

--- a/solution.py
+++ b/solution.py
@@ -24,12 +24,13 @@
 BAND_ROWS = ROWS // IMGS
 SLOTS = OWNERS * MOST
 VIEWS = PAIR_DEV + SLOTS
-CODE_ROWS = 2 * GROUPS + 16
+HALF = GROUPS // 2
+OWN_STEPS = 4
+STEPS = (2, 1, 3)
 TILE = 12
 PART = 4
 UNROLL = 4
 LEVELS = 32700.0
-SCALE_STEPS = 64.0
 
 beta_one = 0.9
 beta_two = 0.999
@@ -93,9 +94,14 @@
     conf_f,
     stage_one,
     stage_two,
-    codes,
-    send_buf,
-    recv_buf,
+    code_one_a,
+    code_one_b,
+    unit_one_a,
+    unit_one_b,
+    inverse_ref,
+    code_two,
+    unit_two,
+    pass_hot,
     meta,
     cu_ref,
     prefix_ref,
@@ -215,7 +221,7 @@
     lax.fori_loop(0, PAIR_DEV * 2 * GROUPS // 64, widen, 0)
     second_load.wait()
 
-    def prepare(view, images, stage, scaled):
+    def prepare(view, images, stage):
         cols = [column([image_pose[i, images[e]] for e in range(PAIR_DEV)]) for i in range(7)]
         rot = rotation(*cols[:4])
         trans = cols[4:]
@@ -228,7 +234,7 @@
         offset = sum(trans[l] * shift[l] for l in range(3))
 
         def body(r, carry):
-            total_sq, total_dot, total_conf = carry
+            total_sq, total_dot, total_conf, largest = carry
             down = r.astype(f32)
             tilt = [slope[j] * down for j in range(4)]
             for part in range(4):
@@ -238,51 +244,82 @@
                 value = base[3][part] + tilt[3]
                 for j in range(3):
                     value = value + (base[j][part] + tilt[j]) * x[j]
-                if scaled:
-                    value = value * weight
+                value = value * weight
+                largest = jnp.maximum(largest, jnp.abs(value))
                 stage[pl.ds(pl.multiple_of((r * 4 + part) * 8, 8), 8), :] = value
                 square = x[0] * (x[0] + lean[0]) + x[1] * (x[1] + lean[1]) + x[2] * (x[2] + lean[2])
                 dot = x[0] * toward[0] + x[1] * toward[1] + x[2] * toward[2]
                 total_sq = total_sq + weight * square
                 total_dot = total_dot + weight * dot
                 total_conf = total_conf + weight
-            return (total_sq, total_dot, total_conf)
-
-        zero = jnp.zeros((8, 128), f32)
-        total_sq, total_dot, total_conf = lax.fori_loop(0, BAND_ROWS, body, (zero, zero, zero))
-        return (total_sq + total_conf * shift_sq, total_dot + total_conf * offset)
-
-    square_two, dot_two = prepare(1, seconds, stage_two, False)
-
-    def encode(e, carry):
-        largest = jnp.full((8, 128), 1e-30, f32)
-        for block in range(BLOCKS):
-            largest = jnp.maximum(largest, jnp.abs(stage_two[pl.ds(block * 64 + e, 8, stride=8), :]))
-        power = jnp.ceil(jnp.log(largest) * (SCALE_STEPS / 0.6931471805599453)).astype(jnp.int32)
-        inverse = LEVELS / jnp.exp(power.astype(f32) * (0.6931471805599453 / SCALE_STEPS))
-        inverse = jnp.concatenate([inverse, inverse], axis=0)
-        for half in range(BLOCKS // 2):
-            value = stage_two[pl.ds(half * 128 + e, 16, stride=8), :] * inverse
-            value = jnp.floor(value + 0.5).astype(jnp.int32).astype(jnp.int16)
-            codes[e, half * 16 : half * 16 + 16, :] = value
-            weight = conf_f[pl.ds(e * 2 * GROUPS + half * 32 + 1, 16, stride=2), :] * 128.0
-            codes[e, GROUPS + half * 16 : GROUPS + half * 16 + 16, :] = weight.astype(jnp.int32).astype(jnp.int16)
-        codes[e, 2 * GROUPS : 2 * GROUPS + 16, :] = jnp.concatenate([power, power], axis=0).astype(jnp.int16)
-        return carry
-
-    lax.fori_loop(0, PAIR_DEV, encode, 0)
-
-    def slot_pair(k, j):
-        wanted = pair_at(k, 1) * MOST + j
-        found = jnp.int32(0)
-        for e in range(1, PAIR_DEV):
-            found = found + jnp.where(order[e] == wanted, e, 0)
-        return found
-
-    for j in range(MOST):
-        recv_buf[0, j] = codes[slot_pair(0, j)]
-
+            return (total_sq, total_dot, total_conf, largest)
+
+        def run(half, sums):
+            tiny = jnp.full((8, 128), 1e-30, f32)
+            start = half * (BAND_ROWS // 2)
+            out = lax.fori_loop(start, start + BAND_ROWS // 2, body, (*sums, tiny))
+            return out[:3], out[3]
+
+        def close(sums):
+            return (sums[0] + sums[2] * shift_sq, sums[1] + sums[2] * offset)
+
+        return run, close
+
+    empty = (jnp.zeros((8, 128), f32),) * 3
+    code_one = (code_one_a, code_one_b)
+    unit_one = (unit_one_a, unit_one_b)
+    run_two, close_two = prepare(1, seconds, stage_two)
+
+    def encode(half, largest):
+        unit_one[half][0] = largest * (1.0 / LEVELS)
+        inverse_ref[...] = LEVELS / largest
+
+        def body(e, carry):
+            inverse = inverse_ref[pl.ds(e, 1), :]
+            for step in range(HALF // 16):
+                place = half * (HALF // 16) + step
+                rows = slice(step * 16, step * 16 + 16)
+                value = stage_two[pl.ds(place * 128 + e, 16, stride=8), :] * inverse
+                code_one[half][0, e, rows, :] = jnp.floor(value + 0.5).astype(jnp.int32).astype(jnp.int16)
+                weight = conf_f[pl.ds(e * 2 * GROUPS + place * 32 + 1, 16, stride=2), :] * 128.0
+                rows = slice(HALF + step * 16, HALF + step * 16 + 16)
+                code_one[half][0, e, rows, :] = weight.astype(jnp.int32).astype(jnp.int16)
+            return carry
+
+        lax.fori_loop(0, PAIR_DEV, body, 0)
+
+    def ahead(axis, d):
+        if axis == 0:
+            return (my_img, ys[d] * ZS + my_z)
+        return (my_img, my_y * ZS + zs[d])
+
+    def bulk_copies(phase, half, d):
+        if phase == 0:
+            refs = (code_one[half], unit_one[half])
+        else:
+            refs = (code_two.at[half], unit_two.at[half])
+        axis = half if phase == 0 else 1 - half
+        source = 0 if phase == 0 else d
+        landing = d if phase == 0 else OWN_STEPS + d
+        sems = (phase * 2 + half) * 4 + d
+        return [
+            pltpu.make_async_remote_copy(
+                src_ref=ref.at[source],
+                dst_ref=ref.at[landing],
+                send_sem=send_sem.at[n, sems],
+                recv_sem=recv_sem.at[n, sems],
+                device_id=ahead(axis, d),
+                device_id_type=MESH,
+            )
+            for n, ref in enumerate(refs)
+        ]
+
+    sums, largest = run_two(0, empty)
+    encode(0, largest)
     pl.semaphore_wait(barrier, CHIPS)
+    for d in STEPS:
+        for copy in bulk_copies(0, 0, d):
+            copy.start()
 
     def meta_copy(k):
         return pltpu.make_async_remote_copy(
@@ -294,31 +331,22 @@
             device_id_type=MESH,
         )
 
-    def slot_copy(k):
-        return pltpu.make_async_remote_copy(
-            src_ref=send_buf.at[k],
-            dst_ref=recv_buf.at[k],
-            send_sem=send_sem.at[k],
-            recv_sem=recv_sem.at[k],
-            device_id=(my_img, pair_at(k, 1)),
-            device_id_type=MESH,
-        )
-
     def start_meta(k, carry):
         meta_copy(k).start()
         return carry
 
-    def start_slots(k, carry):
-        for j in range(MOST):
-            send_buf[k, j] = codes[slot_pair(k, j)]
-        slot_copy(k).start()
-        return carry
-
     lax.fori_loop(1, OWNERS, start_meta, 0)
-    lax.fori_loop(1, OWNERS, start_slots, 0)
-
+    sums, largest = run_two(1, sums)
+    encode(1, largest)
+    for d in STEPS:
+        for copy in bulk_copies(0, 1, d):
+            copy.start()
+    square_two, dot_two = close_two(sums)
     first_load.wait()
-    square_one, dot_one = prepare(0, firsts, stage_one, True)
+    run_one, close_one = prepare(0, firsts, stage_one)
+    sums, largest = run_one(0, empty)
+    sums, largest = run_one(1, sums)
+    square_one, dot_one = close_one(sums)
 
     def depth_of(values):
         return jnp.exp(values.astype(jnp.bfloat16).astype(f32))
@@ -394,7 +422,24 @@
         upto = (listed & (image_row <= v)).astype(jnp.int32)
         end_row = jnp.where(lane == v, jnp.sum(upto, axis=1, keepdims=True), end_row)
     image_row = jnp.minimum(image_row, IMG_DEV - 1)
-    table_ref[...] = jnp.where(sub == 0, image_row, jnp.where(sub == 1, order_row, end_row))
+
+    pass_row = jnp.zeros((8, 128), jnp.int32)
+    for half in range(2):
+        for d in range(4):
+            if half == 0:
+                goal = my_y * ZS + zs[d]
+                source = ((my_y - sub // MOST + YS) % YS) * ZS + my_z
+            else:
+                goal = ys[d] * ZS + my_z
+                source = my_y * ZS + (my_z - sub // MOST + ZS) % ZS
+            match = (from_pair == source) & (code_row == goal * MOST + sub % MOST)
+            chosen = jnp.sum(jnp.where(match, lane % PAIR_DEV, 0), axis=1, keepdims=True)
+            found = jnp.where(lane == sub + (half * 4 + d) * 8, chosen, 0)
+            pass_row = pass_row + jnp.broadcast_to(jnp.sum(found, axis=0, keepdims=True), (8, 128))
+            for v in range(IMG_DEV):
+                hot = jnp.where(match & (local_row == v), 1.0, 0.0)
+                pass_hot[half * 4 + d, v] = jnp.broadcast_to(jnp.sum(hot, axis=1, keepdims=True), (8, 128))
+    table_ref[...] = jnp.where(sub == 0, image_row, jnp.where(sub == 1, order_row, jnp.where(sub == 2, end_row, pass_row)))
     table_copy = pltpu.make_async_copy(table_ref, table, table_sem)
     table_copy.start()
 
@@ -430,43 +475,74 @@
 
     lax.fori_loop(0, BLOCKS, first_sums, 0)
 
-    def take(k, carry):
-        @pl.when(k > 0)
-        def _():
-            slot_copy(k).wait_recv()
-
-        units, hots, images = [], [], []
-        for j in range(MOST):
-            power = recv_buf[k, j, 2 * GROUPS : 2 * GROUPS + 16, :].astype(jnp.int32).astype(f32)
-            unit = jnp.exp(power * (0.6931471805599453 / SCALE_STEPS)) * (1.0 / (LEVELS * 128.0))
-            units.append(unit)
-            slot = PAIR_DEV + k * MOST + j
-            hots.append([hot_ref[v, pl.ds(slot, 1), :] * (1.0 / 128.0) for v in range(IMG_DEV)])
-            images.append(table[0, slot])
-
-        def part(half, totals):
+    def pass_on(half, d):
+        place = d if d > 0 else OWN_STEPS
+        index = half * 4 + d
+        sources = [table[3, index * 8 + n] for n in range(8)]
+        hots = [[pass_hot[index, v, n : n + 1, :] for v in range(IMG_DEV)] for n in range(8)]
+        for n in range(8):
+            unit_two[half, place, n : n + 1, :] = unit_one[half][n // MOST, pl.ds(sources[n], 1), :]
+
+        def body(step, carry):
+            rows = pl.ds(pl.multiple_of(step * 16, 16), 16)
+            weight_rows = pl.ds(pl.multiple_of(HALF + step * 16, 16), 16)
+            totals = [jnp.zeros((16, 128), f32) for v in range(IMG_DEV)]
+            for n in range(8):
+                code_two[half, place, n, rows, :] = code_one[half][n // MOST, sources[n], rows, :]
+                weight = code_one[half][n // MOST, sources[n], weight_rows, :].astype(jnp.int32).astype(f32)
+                for v in range(IMG_DEV):
+                    totals[v] = totals[v] + weight * hots[n][v]
+            for v in range(IMG_DEV):
+                code_two[half, place, 8 + v, rows, :] = totals[v].astype(jnp.int32).astype(jnp.int16)
+            return carry
+
+        lax.fori_loop(0, HALF // 16, body, 0)
+
+    def take(half, d):
+        place = OWN_STEPS + d
+        slots = []
+        for n in range(8):
+            step = n // MOST * 4 + d if half == 0 else d * 4 + n // MOST
+            slots.append(PAIR_DEV + step * MOST + n % MOST)
+        units = [unit_two[half, place, n : n + 1, :] for n in range(8)]
+        images = [table[0, slot] for slot in slots]
+
+        def body(step, totals):
             totals = list(totals)
-            rows = pl.ds(pl.multiple_of(half * 16, 16), 16)
-            weight_rows = pl.ds(pl.multiple_of(GROUPS + half * 16, 16), 16)
-            sums = [weight_sum[v, rows, :] for v in range(IMG_DEV)]
-            for j in range(MOST):
-                value = recv_buf[k, j, rows, :].astype(jnp.int32).astype(f32)
-                weight = recv_buf[k, j, weight_rows, :].astype(jnp.int32).astype(f32)
-                cu = value * units[j] * weight
-                cu_ref[PAIR_DEV + k * MOST + j, rows, :] = cu
-                totals[j] = totals[j] + cu * depth_ref[images[j], rows, :]
-                for v in range(IMG_DEV):
-                    sums[v] = sums[v] + weight * hots[j][v]
+            rows = pl.ds(pl.multiple_of(step * 16, 16), 16)
+            full = pl.ds(pl.multiple_of(half * HALF + step * 16, 16), 16)
+            for n in range(8):
+                cu = code_two[half, place, n, rows, :].astype(jnp.int32).astype(f32) * units[n]
+                cu_ref[slots[n], full, :] = cu
+                cu = cu * depth_ref[images[n], full, :]
+                totals[n] = totals[n] + (cu[0:8] + cu[8:16])
             for v in range(IMG_DEV):
-                weight_sum[v, rows, :] = sums[v]
+                weight = code_two[half, place, 8 + v, rows, :].astype(jnp.int32).astype(f32)
+                weight_sum[v, full, :] = weight_sum[v, full, :] + weight * (1.0 / 128.0)
             return tuple(totals)
 
-        totals = lax.fori_loop(0, BLOCKS // 2, part, tuple(jnp.zeros((16, 128), f32) for j in range(MOST)))
-        for j in range(MOST):
-            inner_ref[pl.ds(PAIR_DEV + k * MOST + j, 1), :] = jnp.sum(totals[j], axis=0, keepdims=True)
-        return carry
-
-    lax.fori_loop(0, OWNERS, take, 0)
+        totals = lax.fori_loop(0, HALF // 16, body, (jnp.zeros((8, 128), f32),) * 8)
+        for n in range(8):
+            total = jnp.sum(totals[n], axis=0, keepdims=True)
+            row = slice(slots[n], slots[n] + 1)
+            inner_ref[row, :] = inner_ref[row, :] + total
+
+    inner_ref[PAIR_DEV:VIEWS, :] = jnp.zeros((SLOTS, 128), f32)
+    for half in range(2):
+        for d in STEPS:
+            for copy in bulk_copies(0, half, d):
+                copy.wait_recv()
+        for d in STEPS:
+            pass_on(half, d)
+            for copy in bulk_copies(1, half, d):
+                copy.start()
+        pass_on(half, 0)
+        take(half, 0)
+    for half in range(2):
+        for d in STEPS:
+            for copy in bulk_copies(1, half, d):
+                copy.wait_recv()
+            take(half, d)
 
     def pair_row(col):
         return jnp.sum(jnp.sum(col, axis=1, keepdims=True) * own_mask, axis=0, keepdims=True)
@@ -612,10 +688,14 @@
 
     def finish(k, carry):
         meta_copy(k).wait_send()
-        slot_copy(k).wait_send()
         return carry
 
     lax.fori_loop(1, OWNERS, finish, 0)
+    for phase in range(2):
+        for half in range(2):
+            for d in STEPS:
+                for copy in bulk_copies(phase, half, d):
+                    copy.wait_send()
     for t in range(ITERS):
         core_copy(t).wait_send()
         for n in range(CHIPS - 1):
@@ -683,9 +763,14 @@
             pltpu.VMEM((PAIR_DEV * GROUPS * 2, 128), f32),
             pltpu.VMEM((PAIR_DEV * GROUPS, 128), f32),
             pltpu.VMEM((PAIR_DEV * GROUPS, 128), f32),
-            pltpu.VMEM((PAIR_DEV, CODE_ROWS, 128), jnp.int16),
-            pltpu.VMEM((OWNERS, MOST, CODE_ROWS, 128), jnp.int16),
-            pltpu.VMEM((OWNERS, MOST, CODE_ROWS, 128), jnp.int16),
+            pltpu.VMEM((4, PAIR_DEV, 2 * HALF, 128), jnp.int16),
+            pltpu.VMEM((4, PAIR_DEV, 2 * HALF, 128), jnp.int16),
+            pltpu.VMEM((4, PAIR_DEV, 128), f32),
+            pltpu.VMEM((4, PAIR_DEV, 128), f32),
+            pltpu.VMEM((PAIR_DEV, 128), f32),
+            pltpu.VMEM((2, 2 * OWN_STEPS, 8 + IMG_DEV, HALF, 128), jnp.int16),
+            pltpu.VMEM((2, 2 * OWN_STEPS, 8, 128), f32),
+            pltpu.VMEM((8, IMG_DEV, 8, 128), f32),
             pltpu.VMEM((OWNERS, 8, 128), jnp.int32),
             pltpu.VMEM((VIEWS, GROUPS, 128), f32),
             pltpu.VMEM((VIEWS + 1, TILE * 8, 128), f32),
@@ -703,8 +788,8 @@
             dma((11,)),
             dma((BLOCKS // TILE, 3)),
             dma,
-            dma((OWNERS,)),
-            dma((OWNERS,)),
+            dma((2, 16)),
+            dma((2, 16)),
             dma((OWNERS,)),
             dma((OWNERS,)),
             dma((ITERS,)),

time: 102 us -> 84.4 us (0.83)
  Pallas kernels: 101 us -> 83.6 us
    pallas_call x1, Pallas kernels: 98.9 us -> 81.5 us  [shards(): pl.pallas_call(kernel, out_shape=(band, band, band, jax.ShapeDtypeStruct(...]
where the time goes in v4:
time: 84.4 us; the launch traced here: 84.3 us
  Pallas kernels  83.6 us (99%)
    pallas_call x1, Pallas kernels, shards(): pl.pallas_call(kernel, out_shape=(band, band, band, jax.ShapeDtypeStruct(...  81.5 us
    pallas_call x1, Pallas kernels, shards(): pl.pallas_call(store, out_shape=(band, band, band, jax.ShapeDtypeStruct((...  2.15 us

profile of v4, /device:TPU:1, one launch (start us, length us, event | category | flops | bytes accessed | tf_op | source)
XLA Modules:
  0.0 84.3 jit_solution(15919171102043003464)
XLA Ops:
  0.6 81.5 %align.1 = (f32[768,128]{1,0:T(8,128)}, f32[768,128]{1,0:T(8,128)}, f32[768,128]{1,0:T(8,128)}, f32[1,8]{1,0:T(1,128)}) custom-call(f32[768,128]{1,0:T(8,128)} %bitcast.40, f32[768,128]{1,0:T(8,128)} %bitcast.41, f32[768,128]{1,0:T(8,128)} %bitcast.42, bf16[6,8,24576]{2,1,0:T(8,128)(2,1)} %bitcast.38, bf16[3072,128]{1,0:T(8,128)(2,1)} %bitcast.39, ...), custom_call_target="tpu_custom_call" | custom-call | tf_op jit(solution)/shard_map/align/pallas_call | solution.py:746
  82.1 2.2 %store.1 = (f32[768,128]{1,0:T(8,128)}, f32[768,128]{1,0:T(8,128)}, f32[768,128]{1,0:T(8,128)}, f32[1,8]{1,0:T(1,128)}) custom-call(f32[768,128]{1,0:T(8,128)} %get-tuple-element.12.log_in, f32[768,128]{1,0:T(8,128)} %get-tuple-element.13.one_in, f32[768,128]{1,0:T(8,128)} %get-tuple-element.14.two_in, f32[1,8]{1,0:T(1,128)} %get-tuple-element.15.scale_in), custom_call_target="tpu_custom_call" | custom-call | tf_op jit(solution)/shard_map/store/pallas_call | solution.py:816

commit v5 on v4

--- a/solution.py
+++ b/solution.py
@@ -29,6 +29,7 @@
 STEPS = (2, 1, 3)
 TILE = 12
 PART = 4
+ADAM = 6
 UNROLL = 4
 LEVELS = 32700.0
 
@@ -105,7 +106,9 @@
     meta,
     cu_ref,
     prefix_ref,
+    state_ref,
     weight_sum,
+    lever_sum,
     depth_ref,
     tau_ref,
     hot_ref,
@@ -359,13 +362,23 @@
 
     def first_depth(block, carry):
         for v in range(IMG_DEV):
-            depth_ref[v, block_rows(block), :] = depth_of(log_ref[image_rows(block, v), :])
+            value = log_ref[image_rows(block, v), :]
+            state_ref[0, v, block_rows(block), :] = value
+            depth_ref[v, block_rows(block), :] = depth_of(value)
         return carry
 
     log_load.wait()
     lax.fori_loop(0, BLOCKS, first_depth, 0)
     for copy in state_loads:
         copy.wait()
+
+    def fold_moments(block, carry):
+        for v in range(IMG_DEV):
+            state_ref[1, v, block_rows(block), :] = one_ref[image_rows(block, v), :]
+            state_ref[2, v, block_rows(block), :] = two_ref[image_rows(block, v), :]
+        return carry
+
+    lax.fori_loop(0, BLOCKS, fold_moments, 0)
 
     own = [[image_pose[i, my_pair * IMG_DEV + min(v, IMG_DEV - 1)] for v in range(8)] for i in range(7)]
     own_cols = [column(own[i]) for i in range(7)]
@@ -573,13 +586,14 @@
             device_id_type=MESH,
         )
 
-    def sum_all(t, tile):
+    def sum_all(t, tile, beside):
         core_buf[t, 0] = tile
         core_copy(t).start()
         core_copy(t).wait_recv()
         chip_buf[t, my_chip] = tile + core_buf[t, 1]
         for n in range(CHIPS - 1):
             chip_copy(t, n, False).start()
+        beside()
         for n in reversed(range(CHIPS - 1)):
             chip_copy(t, n, True).wait_recv()
         parts = [chip_buf[t, n] for n in range(CHIPS)]
@@ -596,6 +610,22 @@
         ]
 
     scale_store = pltpu.make_async_copy(scale_ref, scale_out, load_sem.at[0])
+    def ray_sums():
+        def body(block, carry):
+            down = (block * 2 + sub // 4).astype(f32) + first_row
+            rays_y = (down + 0.5 - ROWS / 2) / COLS
+            rays_x = (((sub % 4) * 128 + lane).astype(f32) + 0.5 - COLS / 2) / COLS
+            length = rays_x * rays_x + rays_y * rays_y + 1.0
+            rows = block_rows(block)
+            for v in range(IMG_DEV):
+                lever = rays_x * tau_ref[0, v : v + 1, :] + rays_y * tau_ref[1, v : v + 1, :] + tau_ref[2, v : v + 1, :]
+                weight = weight_sum[v, rows, :]
+                lever_sum[v, rows, :] = lever * weight
+                weight_sum[v, rows, :] = length * weight
+            return carry
+
+        lax.fori_loop(0, BLOCKS, body, 0)
+
     denominator = None
     for sweep in range(ITERS):
         row = jnp.zeros((8, 128), f32)
@@ -604,7 +634,7 @@
             row = row + jnp.sum(inner_ref[rows, :], axis=1, keepdims=True) * mask_ref[rows, :]
         row = jnp.sum(row, axis=0, keepdims=True) + fixed_row
         two = lax.broadcasted_iota(jnp.int32, (2, 128), 0)
-        total = sum_all(sweep, jnp.where(two == 0, row, square_row))
+        total = sum_all(sweep, jnp.where(two == 0, row, square_row), ray_sums if sweep == 0 else lambda: None)
         if sweep == 0:
             denominator = total[1:2]
         scales = jnp.broadcast_to(total[0:1] / denominator, (8, 128))
@@ -640,38 +670,40 @@
             for m in range(TILE):
                 prefix_ref[0, m * 8 : m * 8 + 8, :] = zero
             lax.fori_loop(0, VIEWS // UNROLL, gather, (zero,) * TILE)
-            def step_adam(n, carry):
-                block = start + n
-                here = pl.ds(pl.multiple_of(n * 8, 8), 8)
-                down = (block * 2 + sub // 4).astype(f32) + first_row
-                rays_y = (down + 0.5 - ROWS / 2) / COLS
-                rays_x = (((sub % 4) * 128 + lane).astype(f32) + 0.5 - COLS / 2) / COLS
-                length = rays_x * rays_x + rays_y * rays_y + 1.0
-                for v in range(IMG_DEV):
-                    depth = depth_ref[v, block_rows(block), :]
-                    lever = rays_x * tau_ref[0, v : v + 1, :] + rays_y * tau_ref[1, v : v + 1, :] + tau_ref[2, v : v + 1, :]
-                    gathered = prefix_ref[table[2, v], here, :]
-                    if v > 0:
-                        gathered = gathered - prefix_ref[table[2, v - 1], here, :]
-                    pull = (depth * length + lever) * weight_sum[v, block_rows(block), :] - gathered
-                    gradient = 2.0 * depth * pull
-                    rows = image_rows(block, v)
-                    old_one = one_ref[rows, :]
-                    old_two = two_ref[rows, :]
-                    old_log = log_ref[rows, :]
-                    new_one = beta_one * old_one + (1 - beta_one) * gradient
-                    new_two = beta_two * old_two + (1 - beta_two) * gradient * gradient
-                    corrected_one = new_one * (1 / bias_one)
-                    corrected_two = new_two * (1 / bias_two)
-                    new_log = old_log - learn_rate * corrected_one / (jnp.sqrt(corrected_two) + adam_eps)
-                    one_ref[rows, :] = new_one
-                    two_ref[rows, :] = new_two
-                    log_ref[rows, :] = new_log
-                    if not last:
-                        depth_ref[v, block_rows(block), :] = depth_of(new_log)
+            def step_adam(step, carry):
+                for m in range(ADAM):
+                    n = step * ADAM + m
+                    block = start + n
+                    here = pl.ds(pl.multiple_of(n * 8, 8), 8)
+                    for v in range(IMG_DEV):
+                        depth = depth_ref[v, block_rows(block), :]
+                        gathered = prefix_ref[table[2, v], here, :]
+                        if v > 0:
+                            gathered = gathered - prefix_ref[table[2, v - 1], here, :]
+                        pull = depth * weight_sum[v, block_rows(block), :] + lever_sum[v, block_rows(block), :] - gathered
+                        half_gradient = depth * pull
+                        rows = block_rows(block)
+                        old_log, old_one, old_two = (state_ref[n, v, rows, :] for n in range(3))
+                        new_one = beta_one * old_one + (2 * (1 - beta_one)) * half_gradient
+                        new_two = beta_two * old_two + (4 * (1 - beta_two)) * (half_gradient * half_gradient)
+                        corrected_two = new_two * (1 / bias_two)
+                        root = corrected_two * lax.rsqrt(corrected_two) + adam_eps
+                        inverse = pl.reciprocal(root, approx=True)
+                        inverse = inverse * (2.0 - root * inverse)
+                        new_log = old_log - (learn_rate / bias_one) * (new_one * inverse)
+                        if last:
+                            rows = image_rows(block, v)
+                            log_ref[rows, :] = new_log
+                            one_ref[rows, :] = new_one
+                            two_ref[rows, :] = new_two
+                        else:
+                            state_ref[0, v, rows, :] = new_log
+                            state_ref[1, v, rows, :] = new_one
+                            state_ref[2, v, rows, :] = new_two
+                            depth_ref[v, rows, :] = depth_of(new_log)
                 return carry
 
-            lax.fori_loop(0, TILE, step_adam, 0)
+            lax.fori_loop(0, TILE // ADAM, step_adam, 0)
             if last:
                 for copy in stores(tile_id):
                     copy.start()
@@ -774,6 +806,8 @@
             pltpu.VMEM((OWNERS, 8, 128), jnp.int32),
             pltpu.VMEM((VIEWS, GROUPS, 128), f32),
             pltpu.VMEM((VIEWS + 1, TILE * 8, 128), f32),
+            pltpu.VMEM((3, IMG_DEV, GROUPS, 128), f32),
+            pltpu.VMEM((IMG_DEV, GROUPS, 128), f32),
             pltpu.VMEM((IMG_DEV, GROUPS, 128), f32),
             pltpu.VMEM((IMG_DEV, GROUPS, 128), f32),
             pltpu.VMEM((3, 8, 128), f32),

time: 84.4 us -> 82.4 us (0.976)
  Pallas kernels: 83.6 us -> 81.6 us
    pallas_call x1, Pallas kernels: 81.5 us -> 79.5 us  [shards(): pl.pallas_call(kernel, out_shape=(band, band, band, jax.ShapeDtypeStruct(...]
where the time goes in v5:
time: 82.4 us; the launch traced here: 82.3 us
  Pallas kernels  81.6 us (99%)
    pallas_call x1, Pallas kernels, shards(): pl.pallas_call(kernel, out_shape=(band, band, band, jax.ShapeDtypeStruct(...  79.5 us
    pallas_call x1, Pallas kernels, shards(): pl.pallas_call(store, out_shape=(band, band, band, jax.ShapeDtypeStruct((...  2.15 us

profile of v5, /device:TPU:1, one launch (start us, length us, event | category | flops | bytes accessed | tf_op | source)
XLA Modules:
  0.0 82.3 jit_solution(1097699489723001443)
XLA Ops:
  0.6 79.5 %align.1 = (f32[768,128]{1,0:T(8,128)}, f32[768,128]{1,0:T(8,128)}, f32[768,128]{1,0:T(8,128)}, f32[1,8]{1,0:T(1,128)}) custom-call(f32[768,128]{1,0:T(8,128)} %bitcast.40, f32[768,128]{1,0:T(8,128)} %bitcast.41, f32[768,128]{1,0:T(8,128)} %bitcast.42, bf16[6,8,24576]{2,1,0:T(8,128)(2,1)} %bitcast.38, bf16[3072,128]{1,0:T(8,128)(2,1)} %bitcast.39, ...), custom_call_target="tpu_custom_call" | custom-call | tf_op jit(solution)/shard_map/align/pallas_call | solution.py:778
  80.1 2.2 %store.1 = (f32[768,128]{1,0:T(8,128)}, f32[768,128]{1,0:T(8,128)}, f32[768,128]{1,0:T(8,128)}, f32[1,8]{1,0:T(1,128)}) custom-call(f32[768,128]{1,0:T(8,128)} %get-tuple-element.12.log_in, f32[768,128]{1,0:T(8,128)} %get-tuple-element.13.one_in, f32[768,128]{1,0:T(8,128)} %get-tuple-element.14.two_in, f32[1,8]{1,0:T(1,128)} %get-tuple-element.15.scale_in), custom_call_target="tpu_custom_call" | custom-call | tf_op jit(solution)/shard_map/store/pallas_call | solution.py:850

commit v6 on v5

--- a/solution.py
+++ b/solution.py
@@ -24,7 +24,9 @@
 BAND_ROWS = ROWS // IMGS
 SLOTS = OWNERS * MOST
 VIEWS = PAIR_DEV + SLOTS
-HALF = GROUPS // 2
+UNITS = 4
+CHUNK = GROUPS // UNITS
+UNIT_ROWS = BAND_ROWS // UNITS
 OWN_STEPS = 4
 STEPS = (2, 1, 3)
 TILE = 12
@@ -97,11 +99,16 @@
     stage_two,
     code_one_a,
     code_one_b,
+    code_one_c,
+    code_one_d,
     unit_one_a,
     unit_one_b,
+    unit_one_c,
+    unit_one_d,
     inverse_ref,
     code_two,
     unit_two,
+    part_ref,
     pass_hot,
     meta,
     cu_ref,
@@ -122,8 +129,14 @@
     load_sem,
     store_sem,
     table_sem,
-    send_sem,
-    recv_sem,
+    one_send,
+    one_recv,
+    scale_send,
+    scale_recv,
+    two_send,
+    two_recv,
+    pass_send,
+    pass_recv,
     meta_send,
     meta_recv,
     core_send,
@@ -257,10 +270,10 @@
                 total_conf = total_conf + weight
             return (total_sq, total_dot, total_conf, largest)
 
-        def run(half, sums):
+        def run(unit, sums):
             tiny = jnp.full((8, 128), 1e-30, f32)
-            start = half * (BAND_ROWS // 2)
-            out = lax.fori_loop(start, start + BAND_ROWS // 2, body, (*sums, tiny))
+            start = unit * UNIT_ROWS
+            out = lax.fori_loop(start, start + UNIT_ROWS, body, (*sums, tiny))
             return out[:3], out[3]
 
         def close(sums):
@@ -269,24 +282,24 @@
         return run, close
 
     empty = (jnp.zeros((8, 128), f32),) * 3
-    code_one = (code_one_a, code_one_b)
-    unit_one = (unit_one_a, unit_one_b)
+    code_one = (code_one_a, code_one_b, code_one_c, code_one_d)
+    unit_one = (unit_one_a, unit_one_b, unit_one_c, unit_one_d)
     run_two, close_two = prepare(1, seconds, stage_two)
 
-    def encode(half, largest):
-        unit_one[half][0] = largest * (1.0 / LEVELS)
+    def encode(unit, largest):
+        unit_one[unit][0] = largest * (1.0 / LEVELS)
         inverse_ref[...] = LEVELS / largest
 
         def body(e, carry):
             inverse = inverse_ref[pl.ds(e, 1), :]
-            for step in range(HALF // 16):
-                place = half * (HALF // 16) + step
+            for step in range(CHUNK // 16):
+                place = unit * (CHUNK // 16) + step
                 rows = slice(step * 16, step * 16 + 16)
                 value = stage_two[pl.ds(place * 128 + e, 16, stride=8), :] * inverse
-                code_one[half][0, e, rows, :] = jnp.floor(value + 0.5).astype(jnp.int32).astype(jnp.int16)
+                code_one[unit][0, e, rows, :] = jnp.floor(value + 0.5).astype(jnp.int32).astype(jnp.int16)
                 weight = conf_f[pl.ds(e * 2 * GROUPS + place * 32 + 1, 16, stride=2), :] * 128.0
-                rows = slice(HALF + step * 16, HALF + step * 16 + 16)
-                code_one[half][0, e, rows, :] = weight.astype(jnp.int32).astype(jnp.int16)
+                rows = slice(CHUNK + step * 16, CHUNK + step * 16 + 16)
+                code_one[unit][0, e, rows, :] = weight.astype(jnp.int32).astype(jnp.int16)
             return carry
 
         lax.fori_loop(0, PAIR_DEV, body, 0)
@@ -296,33 +309,60 @@
             return (my_img, ys[d] * ZS + my_z)
         return (my_img, my_y * ZS + zs[d])
 
-    def bulk_copies(phase, half, d):
-        if phase == 0:
-            refs = (code_one[half], unit_one[half])
-        else:
-            refs = (code_two.at[half], unit_two.at[half])
-        axis = half if phase == 0 else 1 - half
-        source = 0 if phase == 0 else d
-        landing = d if phase == 0 else OWN_STEPS + d
-        sems = (phase * 2 + half) * 4 + d
+    def remote(src, dst, sems, place, device):
+        return pltpu.make_async_remote_copy(
+            src_ref=src,
+            dst_ref=dst,
+            send_sem=sems[0].at[place],
+            recv_sem=sems[1].at[place],
+            device_id=device,
+            device_id_type=MESH,
+        )
+
+    def near_copies(unit):
         return [
-            pltpu.make_async_remote_copy(
-                src_ref=ref.at[source],
-                dst_ref=ref.at[landing],
-                send_sem=send_sem.at[n, sems],
-                recv_sem=recv_sem.at[n, sems],
-                device_id=ahead(axis, d),
-                device_id_type=MESH,
+            remote(code_one[unit].at[0], code_one[unit].at[d], (one_send, one_recv), unit * 4 + d, ahead(unit % 2, d))
+            for d in (1, 3)
+        ]
+
+    def far_copies(unit):
+        half = PAIR_DEV // 2
+        return [
+            remote(
+                code_one[unit].at[d, part], code_one[unit].at[2, part], (one_send, one_recv), unit * 4 + n, ahead(unit % 2, d)
             )
-            for n, ref in enumerate(refs)
+            for d, n, part in ((1, 0, pl.ds(0, half)), (3, 2, pl.ds(half, half)))
         ]
 
-    sums, largest = run_two(0, empty)
-    encode(0, largest)
-    pl.semaphore_wait(barrier, CHIPS)
-    for d in STEPS:
-        for copy in bulk_copies(0, 0, d):
+    def scale_copies(unit):
+        return [
+            remote(unit_one[unit].at[0], unit_one[unit].at[d], (scale_send, scale_recv), unit * 4 + d, ahead(unit % 2, d))
+            for d in STEPS
+        ]
+
+    def slot_copies(unit, d):
+        place = unit * 4 + d
+        to = ahead(1 - unit % 2, d)
+        return [
+            remote(code_two.at[unit, d], code_two.at[unit, OWN_STEPS + d], (two_send, two_recv), place, to),
+            remote(unit_two.at[unit, d], unit_two.at[unit, OWN_STEPS + d], (pass_send, pass_recv), place, to),
+        ]
+
+    def send(unit, sums):
+        sums, largest = run_two(unit, sums)
+        encode(unit, largest)
+        if unit == 0:
+            pl.semaphore_wait(barrier, CHIPS)
+        for copy in near_copies(unit) + scale_copies(unit):
             copy.start()
+        return sums
+
+    def hand_on(unit):
+        for arrived, copy in zip(near_copies(unit), far_copies(unit)):
+            arrived.wait_recv()
+            copy.start()
+
+    sums = send(0, empty)
 
     def meta_copy(k):
         return pltpu.make_async_remote_copy(
@@ -339,16 +379,14 @@
         return carry
 
     lax.fori_loop(1, OWNERS, start_meta, 0)
-    sums, largest = run_two(1, sums)
-    encode(1, largest)
-    for d in STEPS:
-        for copy in bulk_copies(0, 1, d):
-            copy.start()
+    for unit in range(1, UNITS):
+        sums = send(unit, sums)
     square_two, dot_two = close_two(sums)
     first_load.wait()
     run_one, close_one = prepare(0, firsts, stage_one)
-    sums, largest = run_one(0, empty)
-    sums, largest = run_one(1, sums)
+    sums = empty
+    for unit in range(UNITS):
+        sums, largest = run_one(unit, sums)
     square_one, dot_one = close_one(sums)
 
     def depth_of(values):
@@ -379,6 +417,9 @@
         return carry
 
     lax.fori_loop(0, BLOCKS, fold_moments, 0)
+
+    for unit in range(min(2, UNITS)):
+        hand_on(unit)
 
     own = [[image_pose[i, my_pair * IMG_DEV + min(v, IMG_DEV - 1)] for v in range(8)] for i in range(7)]
     own_cols = [column(own[i]) for i in range(7)]
@@ -488,74 +529,75 @@
 
     lax.fori_loop(0, BLOCKS, first_sums, 0)
 
-    def pass_on(half, d):
+    def pass_on(unit, d):
         place = d if d > 0 else OWN_STEPS
-        index = half * 4 + d
+        index = unit % 2 * 4 + d
         sources = [table[3, index * 8 + n] for n in range(8)]
         hots = [[pass_hot[index, v, n : n + 1, :] for v in range(IMG_DEV)] for n in range(8)]
         for n in range(8):
-            unit_two[half, place, n : n + 1, :] = unit_one[half][n // MOST, pl.ds(sources[n], 1), :]
+            unit_two[unit, place, n : n + 1, :] = unit_one[unit][n // MOST, pl.ds(sources[n], 1), :]
 
         def body(step, carry):
             rows = pl.ds(pl.multiple_of(step * 16, 16), 16)
-            weight_rows = pl.ds(pl.multiple_of(HALF + step * 16, 16), 16)
+            weight_rows = pl.ds(pl.multiple_of(CHUNK + step * 16, 16), 16)
             totals = [jnp.zeros((16, 128), f32) for v in range(IMG_DEV)]
             for n in range(8):
-                code_two[half, place, n, rows, :] = code_one[half][n // MOST, sources[n], rows, :]
-                weight = code_one[half][n // MOST, sources[n], weight_rows, :].astype(jnp.int32).astype(f32)
+                code_two[unit, place, n, rows, :] = code_one[unit][n // MOST, sources[n], rows, :]
+                weight = code_one[unit][n // MOST, sources[n], weight_rows, :].astype(jnp.int32).astype(f32)
                 for v in range(IMG_DEV):
                     totals[v] = totals[v] + weight * hots[n][v]
             for v in range(IMG_DEV):
-                code_two[half, place, 8 + v, rows, :] = totals[v].astype(jnp.int32).astype(jnp.int16)
+                code_two[unit, place, 8 + v, rows, :] = totals[v].astype(jnp.int32).astype(jnp.int16)
             return carry
 
-        lax.fori_loop(0, HALF // 16, body, 0)
-
-    def take(half, d):
+        lax.fori_loop(0, CHUNK // 16, body, 0)
+
+    def take(unit, d):
         place = OWN_STEPS + d
         slots = []
         for n in range(8):
-            step = n // MOST * 4 + d if half == 0 else d * 4 + n // MOST
+            step = n // MOST * 4 + d if unit % 2 == 0 else d * 4 + n // MOST
             slots.append(PAIR_DEV + step * MOST + n % MOST)
-        units = [unit_two[half, place, n : n + 1, :] for n in range(8)]
+        units = [unit_two[unit, place, n : n + 1, :] for n in range(8)]
         images = [table[0, slot] for slot in slots]
 
         def body(step, totals):
             totals = list(totals)
             rows = pl.ds(pl.multiple_of(step * 16, 16), 16)
-            full = pl.ds(pl.multiple_of(half * HALF + step * 16, 16), 16)
+            full = pl.ds(pl.multiple_of(unit * CHUNK + step * 16, 16), 16)
             for n in range(8):
-                cu = code_two[half, place, n, rows, :].astype(jnp.int32).astype(f32) * units[n]
+                cu = code_two[unit, place, n, rows, :].astype(jnp.int32).astype(f32) * units[n]
                 cu_ref[slots[n], full, :] = cu
                 cu = cu * depth_ref[images[n], full, :]
                 totals[n] = totals[n] + (cu[0:8] + cu[8:16])
             for v in range(IMG_DEV):
-                weight = code_two[half, place, 8 + v, rows, :].astype(jnp.int32).astype(f32)
+                weight = code_two[unit, place, 8 + v, rows, :].astype(jnp.int32).astype(f32)
                 weight_sum[v, full, :] = weight_sum[v, full, :] + weight * (1.0 / 128.0)
             return tuple(totals)
 
-        totals = lax.fori_loop(0, HALF // 16, body, (jnp.zeros((8, 128), f32),) * 8)
+        totals = lax.fori_loop(0, CHUNK // 16, body, (jnp.zeros((8, 128), f32),) * 8)
         for n in range(8):
-            total = jnp.sum(totals[n], axis=0, keepdims=True)
-            row = slice(slots[n], slots[n] + 1)
-            inner_ref[row, :] = inner_ref[row, :] + total
-
-    inner_ref[PAIR_DEV:VIEWS, :] = jnp.zeros((SLOTS, 128), f32)
-    for half in range(2):
+            row = slice(slots[n] - PAIR_DEV, slots[n] - PAIR_DEV + 1)
+            part_ref[unit, row, :] = jnp.sum(totals[n], axis=0, keepdims=True)
+
+    for unit in range(2, UNITS):
+        hand_on(unit)
+    for unit in range(UNITS):
+        for copy in far_copies(unit) + scale_copies(unit):
+            copy.wait_recv()
         for d in STEPS:
-            for copy in bulk_copies(0, half, d):
+            pass_on(unit, d)
+            for copy in slot_copies(unit, d):
+                copy.start()
+    for unit in range(UNITS):
+        pass_on(unit, 0)
+        take(unit, 0)
+    for unit in range(UNITS):
+        for d in STEPS:
+            for copy in slot_copies(unit, d):
                 copy.wait_recv()
-        for d in STEPS:
-            pass_on(half, d)
-            for copy in bulk_copies(1, half, d):
-                copy.start()
-        pass_on(half, 0)
-        take(half, 0)
-    for half in range(2):
-        for d in STEPS:
-            for copy in bulk_copies(1, half, d):
-                copy.wait_recv()
-            take(half, d)
+            take(unit, d)
+    inner_ref[PAIR_DEV:VIEWS, :] = sum(part_ref[unit] for unit in range(1, UNITS)) + part_ref[0]
 
     def pair_row(col):
         return jnp.sum(jnp.sum(col, axis=1, keepdims=True) * own_mask, axis=0, keepdims=True)
@@ -723,11 +765,12 @@
         return carry
 
     lax.fori_loop(1, OWNERS, finish, 0)
-    for phase in range(2):
-        for half in range(2):
-            for d in STEPS:
-                for copy in bulk_copies(phase, half, d):
-                    copy.wait_send()
+    for unit in range(UNITS):
+        for copy in near_copies(unit) + far_copies(unit) + scale_copies(unit):
+            copy.wait_send()
+        for d in STEPS:
+            for copy in slot_copies(unit, d):
+                copy.wait_send()
     for t in range(ITERS):
         core_copy(t).wait_send()
         for n in range(CHIPS - 1):
@@ -795,13 +838,12 @@
             pltpu.VMEM((PAIR_DEV * GROUPS * 2, 128), f32),
             pltpu.VMEM((PAIR_DEV * GROUPS, 128), f32),
             pltpu.VMEM((PAIR_DEV * GROUPS, 128), f32),
-            pltpu.VMEM((4, PAIR_DEV, 2 * HALF, 128), jnp.int16),
-            pltpu.VMEM((4, PAIR_DEV, 2 * HALF, 128), jnp.int16),
-            pltpu.VMEM((4, PAIR_DEV, 128), f32),
-            pltpu.VMEM((4, PAIR_DEV, 128), f32),
+            *(pltpu.VMEM((4, PAIR_DEV, 2 * CHUNK, 128), jnp.int16) for unit in range(4)),
+            *(pltpu.VMEM((4, PAIR_DEV, 128), f32) for unit in range(4)),
             pltpu.VMEM((PAIR_DEV, 128), f32),
-            pltpu.VMEM((2, 2 * OWN_STEPS, 8 + IMG_DEV, HALF, 128), jnp.int16),
-            pltpu.VMEM((2, 2 * OWN_STEPS, 8, 128), f32),
+            pltpu.VMEM((UNITS, 2 * OWN_STEPS, 8 + IMG_DEV, CHUNK, 128), jnp.int16),
+            pltpu.VMEM((UNITS, 2 * OWN_STEPS, 8, 128), f32),
+            pltpu.VMEM((UNITS, SLOTS, 128), f32),
             pltpu.VMEM((8, IMG_DEV, 8, 128), f32),
             pltpu.VMEM((OWNERS, 8, 128), jnp.int32),
             pltpu.VMEM((VIEWS, GROUPS, 128), f32),
@@ -822,8 +864,7 @@
             dma((11,)),
             dma((BLOCKS // TILE, 3)),
             dma,
-            dma((2, 16)),
-            dma((2, 16)),
+            *(dma((UNITS * 4,)) for kind in range(8)),
             dma((OWNERS,)),
             dma((OWNERS,)),
             dma((ITERS,)),

time: 82.4 us -> 73.7 us (0.89)
  Pallas kernels: 81.6 us -> 72.9 us
    pallas_call x1, Pallas kernels: 79.5 us -> 70.8 us  [shards(): pl.pallas_call(kernel, out_shape=(band, band, band, jax.ShapeDtypeStruct(...]
where the time goes in v6:
time: 73.7 us; the launch traced here: 73.5 us
  Pallas kernels  72.9 us (99%)
    pallas_call x1, Pallas kernels, shards(): pl.pallas_call(kernel, out_shape=(band, band, band, jax.ShapeDtypeStruct(...  70.8 us
    pallas_call x1, Pallas kernels, shards(): pl.pallas_call(store, out_shape=(band, band, band, jax.ShapeDtypeStruct((...  2.15 us

profile of v6, /device:TPU:1, one launch (start us, length us, event | category | flops | bytes accessed | tf_op | source)
XLA Modules:
  0.0 73.5 jit_solution(13557269884214756354)
XLA Ops:
  0.6 70.8 %align.1 = (f32[768,128]{1,0:T(8,128)}, f32[768,128]{1,0:T(8,128)}, f32[768,128]{1,0:T(8,128)}, f32[1,8]{1,0:T(1,128)}) custom-call(f32[768,128]{1,0:T(8,128)} %bitcast.40, f32[768,128]{1,0:T(8,128)} %bitcast.41, f32[768,128]{1,0:T(8,128)} %bitcast.42, bf16[6,8,24576]{2,1,0:T(8,128)(2,1)} %bitcast.38, bf16[3072,128]{1,0:T(8,128)(2,1)} %bitcast.39, ...), custom_call_target="tpu_custom_call" | custom-call | tf_op jit(solution)/shard_map/align/pallas_call | solution.py:821
  71.4 2.2 %store.1 = (f32[768,128]{1,0:T(8,128)}, f32[768,128]{1,0:T(8,128)}, f32[768,128]{1,0:T(8,128)}, f32[1,8]{1,0:T(1,128)}) custom-call(f32[768,128]{1,0:T(8,128)} %get-tuple-element.12.log_in, f32[768,128]{1,0:T(8,128)} %get-tuple-element.13.one_in, f32[768,128]{1,0:T(8,128)} %get-tuple-element.14.two_in, f32[1,8]{1,0:T(1,128)} %get-tuple-element.15.scale_in), custom_call_target="tpu_custom_call" | custom-call | tf_op jit(solution)/shard_map/store/pallas_call | solution.py:891

commit v7 on v6

--- a/solution.py
+++ b/solution.py
@@ -32,7 +32,7 @@
 TILE = 12
 PART = 4
 ADAM = 6
-UNROLL = 4
+UNROLL = 8
 LEVELS = 32700.0
 
 beta_one = 0.9
@@ -97,14 +97,6 @@
     conf_f,
     stage_one,
     stage_two,
-    code_one_a,
-    code_one_b,
-    code_one_c,
-    code_one_d,
-    unit_one_a,
-    unit_one_b,
-    unit_one_c,
-    unit_one_d,
     inverse_ref,
     code_two,
     unit_two,
@@ -143,6 +135,7 @@
     core_recv,
     chip_send,
     chip_recv,
+    *per_unit,
 ):
     def load(n, src, dst):
         copy = pltpu.make_async_copy(src, dst, load_sem.at[n])
@@ -282,8 +275,7 @@
         return run, close
 
     empty = (jnp.zeros((8, 128), f32),) * 3
-    code_one = (code_one_a, code_one_b, code_one_c, code_one_d)
-    unit_one = (unit_one_a, unit_one_b, unit_one_c, unit_one_d)
+    code_one, unit_one = per_unit[:UNITS], per_unit[UNITS:]
     run_two, close_two = prepare(1, seconds, stage_two)
 
     def encode(unit, largest):
@@ -382,13 +374,6 @@
     for unit in range(1, UNITS):
         sums = send(unit, sums)
     square_two, dot_two = close_two(sums)
-    first_load.wait()
-    run_one, close_one = prepare(0, firsts, stage_one)
-    sums = empty
-    for unit in range(UNITS):
-        sums, largest = run_one(unit, sums)
-    square_one, dot_one = close_one(sums)
-
     def depth_of(values):
         return jnp.exp(values.astype(jnp.bfloat16).astype(f32))
 
@@ -405,22 +390,73 @@
             depth_ref[v, block_rows(block), :] = depth_of(value)
         return carry
 
-    log_load.wait()
-    lax.fori_loop(0, BLOCKS, first_depth, 0)
-    for copy in state_loads:
-        copy.wait()
-
     def fold_moments(block, carry):
         for v in range(IMG_DEV):
             state_ref[1, v, block_rows(block), :] = one_ref[image_rows(block, v), :]
             state_ref[2, v, block_rows(block), :] = two_ref[image_rows(block, v), :]
         return carry
 
-    lax.fori_loop(0, BLOCKS, fold_moments, 0)
-
-    for unit in range(min(2, UNITS)):
-        hand_on(unit)
-
+    def pass_on(unit, d):
+        place = d if d > 0 else OWN_STEPS
+        index = unit % 2 * 4 + d
+        sources = [table[3, index * 8 + n] for n in range(8)]
+        hots = [[pass_hot[index, v, n : n + 1, :] for v in range(IMG_DEV)] for n in range(8)]
+        for n in range(8):
+            unit_two[unit, place, n : n + 1, :] = unit_one[unit][n // MOST, pl.ds(sources[n], 1), :]
+
+        def body(step, carry):
+            rows = pl.ds(pl.multiple_of(step * 16, 16), 16)
+            weight_rows = pl.ds(pl.multiple_of(CHUNK + step * 16, 16), 16)
+            totals = [jnp.zeros((16, 128), f32) for v in range(IMG_DEV)]
+            for n in range(8):
+                code_two[unit, place, n, rows, :] = code_one[unit][n // MOST, sources[n], rows, :]
+                weight = code_one[unit][n // MOST, sources[n], weight_rows, :].astype(jnp.int32).astype(f32)
+                for v in range(IMG_DEV):
+                    totals[v] = totals[v] + weight * hots[n][v]
+            for v in range(IMG_DEV):
+                code_two[unit, place, 8 + v, rows, :] = totals[v].astype(jnp.int32).astype(jnp.int16)
+            return carry
+
+        for step in range(CHUNK // 16):
+            body(step, 0)
+
+    def take(unit, d):
+        place = OWN_STEPS + d
+        slots = []
+        for n in range(8):
+            step = n // MOST * 4 + d if unit % 2 == 0 else d * 4 + n // MOST
+            slots.append(PAIR_DEV + step * MOST + n % MOST)
+        units = [unit_two[unit, place, n : n + 1, :] for n in range(8)]
+        images = [table[0, slot] for slot in slots]
+
+        def body(step, totals):
+            totals = list(totals)
+            rows = pl.ds(pl.multiple_of(step * 16, 16), 16)
+            full = pl.ds(pl.multiple_of(unit * CHUNK + step * 16, 16), 16)
+            for n in range(8):
+                cu = code_two[unit, place, n, rows, :].astype(jnp.int32).astype(f32) * units[n]
+                cu_ref[slots[n], full, :] = cu
+                cu = cu * depth_ref[images[n], full, :]
+                totals[n] = totals[n] + (cu[0:8] + cu[8:16])
+            for v in range(IMG_DEV):
+                weight = code_two[unit, place, 8 + v, rows, :].astype(jnp.int32).astype(f32)
+                weight_sum[v, full, :] = weight_sum[v, full, :] + weight * (1.0 / 128.0)
+            return tuple(totals)
+
+        totals = (jnp.zeros((8, 128), f32),) * 8
+        for step in range(CHUNK // 16):
+            totals = body(step, totals)
+        for n in range(8):
+            row = slice(slots[n] - PAIR_DEV, slots[n] - PAIR_DEV + 1)
+            part_ref[unit, row, :] = jnp.sum(totals[n], axis=0, keepdims=True)
+
+    def relay(unit):
+        for copy in far_copies(unit) + scale_copies(unit):
+            copy.wait_recv()
+        for d in STEPS:
+            pass_on(unit, d)
+            for copy in slot_copies(unit, d):
+                copy.start()
     own = [[image_pose[i, my_pair * IMG_DEV + min(v, IMG_DEV - 1)] for v in range(8)] for i in range(7)]
     own_cols = [column(own[i]) for i in range(7)]
     own_rot = rotation(*own_cols[:4])
@@ -497,13 +533,39 @@
     table_copy = pltpu.make_async_copy(table_ref, table, table_sem)
     table_copy.start()
 
+    first_load.wait()
+    run_one, close_one = prepare(0, firsts, stage_one)
+    sums = empty
+    for unit in range(UNITS):
+        sums, largest = run_one(unit, sums)
+    square_one, dot_one = close_one(sums)
+
+    hand_on(0)
+    hand_on(1)
+    log_load.wait()
+    lax.fori_loop(0, BLOCKS, first_depth, 0)
+    for copy in state_loads:
+        copy.wait()
+
+    lax.fori_loop(0, BLOCKS, fold_moments, 0)
+
+    for unit in range(2, UNITS):
+        hand_on(unit)
+    table_copy.wait()
+    for unit in range(UNITS):
+        relay(unit)
+
     def first_copy(e, carry):
         for block in range(BLOCKS):
             cu_ref[e, block * 8 : block * 8 + 8, :] = stage_one[pl.ds(block * 64 + e, 8, stride=8), :]
         return carry
 
     lax.fori_loop(0, PAIR_DEV, first_copy, 0)
-    table_copy.wait()
+
+    def dot_views(step, carry):
+        for n in range(4):
+            dot_view(step * 4 + n, carry)
+        return carry
 
     def dot_view(r, carry):
         v = table[0, r]
@@ -515,7 +577,7 @@
         inner_ref[pl.ds(r, 1), :] = jnp.sum(total, axis=0, keepdims=True)
         return carry
 
-    lax.fori_loop(0, PAIR_DEV, dot_view, 0)
+    lax.fori_loop(0, PAIR_DEV // 4, dot_views, 0)
 
     def first_sums(block, carry):
         sums = [jnp.zeros((8, 128), f32) for v in range(IMG_DEV)]
@@ -529,66 +591,6 @@
 
     lax.fori_loop(0, BLOCKS, first_sums, 0)
 
-    def pass_on(unit, d):
-        place = d if d > 0 else OWN_STEPS
-        index = unit % 2 * 4 + d
-        sources = [table[3, index * 8 + n] for n in range(8)]
-        hots = [[pass_hot[index, v, n : n + 1, :] for v in range(IMG_DEV)] for n in range(8)]
-        for n in range(8):
-            unit_two[unit, place, n : n + 1, :] = unit_one[unit][n // MOST, pl.ds(sources[n], 1), :]
-
-        def body(step, carry):
-            rows = pl.ds(pl.multiple_of(step * 16, 16), 16)
-            weight_rows = pl.ds(pl.multiple_of(CHUNK + step * 16, 16), 16)
-            totals = [jnp.zeros((16, 128), f32) for v in range(IMG_DEV)]
-            for n in range(8):
-                code_two[unit, place, n, rows, :] = code_one[unit][n // MOST, sources[n], rows, :]
-                weight = code_one[unit][n // MOST, sources[n], weight_rows, :].astype(jnp.int32).astype(f32)
-                for v in range(IMG_DEV):
-                    totals[v] = totals[v] + weight * hots[n][v]
-            for v in range(IMG_DEV):
-                code_two[unit, place, 8 + v, rows, :] = totals[v].astype(jnp.int32).astype(jnp.int16)
-            return carry
-
-        lax.fori_loop(0, CHUNK // 16, body, 0)
-
-    def take(unit, d):
-        place = OWN_STEPS + d
-        slots = []
-        for n in range(8):
-            step = n // MOST * 4 + d if unit % 2 == 0 else d * 4 + n // MOST
-            slots.append(PAIR_DEV + step * MOST + n % MOST)
-        units = [unit_two[unit, place, n : n + 1, :] for n in range(8)]
-        images = [table[0, slot] for slot in slots]
-
-        def body(step, totals):
-            totals = list(totals)
-            rows = pl.ds(pl.multiple_of(step * 16, 16), 16)
-            full = pl.ds(pl.multiple_of(unit * CHUNK + step * 16, 16), 16)
-            for n in range(8):
-                cu = code_two[unit, place, n, rows, :].astype(jnp.int32).astype(f32) * units[n]
-                cu_ref[slots[n], full, :] = cu
-                cu = cu * depth_ref[images[n], full, :]
-                totals[n] = totals[n] + (cu[0:8] + cu[8:16])
-            for v in range(IMG_DEV):
-                weight = code_two[unit, place, 8 + v, rows, :].astype(jnp.int32).astype(f32)
-                weight_sum[v, full, :] = weight_sum[v, full, :] + weight * (1.0 / 128.0)
-            return tuple(totals)
-
-        totals = lax.fori_loop(0, CHUNK // 16, body, (jnp.zeros((8, 128), f32),) * 8)
-        for n in range(8):
-            row = slice(slots[n] - PAIR_DEV, slots[n] - PAIR_DEV + 1)
-            part_ref[unit, row, :] = jnp.sum(totals[n], axis=0, keepdims=True)
-
-    for unit in range(2, UNITS):
-        hand_on(unit)
-    for unit in range(UNITS):
-        for copy in far_copies(unit) + scale_copies(unit):
-            copy.wait_recv()
-        for d in STEPS:
-            pass_on(unit, d)
-            for copy in slot_copies(unit, d):
-                copy.start()
     for unit in range(UNITS):
         pass_on(unit, 0)
         take(unit, 0)
@@ -753,7 +755,7 @@
 
         lax.fori_loop(0, BLOCKS // TILE, update, 0)
         if not last:
-            lax.fori_loop(0, VIEWS, dot_view, 0)
+            lax.fori_loop(0, VIEWS // 4, dot_views, 0)
 
     scale_store.wait()
     for tile_id in range(BLOCKS // TILE):
@@ -838,8 +840,6 @@
             pltpu.VMEM((PAIR_DEV * GROUPS * 2, 128), f32),
             pltpu.VMEM((PAIR_DEV * GROUPS, 128), f32),
             pltpu.VMEM((PAIR_DEV * GROUPS, 128), f32),
-            *(pltpu.VMEM((4, PAIR_DEV, 2 * CHUNK, 128), jnp.int16) for unit in range(4)),
-            *(pltpu.VMEM((4, PAIR_DEV, 128), f32) for unit in range(4)),
             pltpu.VMEM((PAIR_DEV, 128), f32),
             pltpu.VMEM((UNITS, 2 * OWN_STEPS, 8 + IMG_DEV, CHUNK, 128), jnp.int16),
             pltpu.VMEM((UNITS, 2 * OWN_STEPS, 8, 128), f32),
@@ -871,6 +871,8 @@
             dma((ITERS,)),
             dma((ITERS, CHIPS)),
             dma((ITERS, CHIPS)),
+            *(pltpu.VMEM((4, PAIR_DEV, 2 * CHUNK, 128), jnp.int16) for unit in range(UNITS)),
+            *(pltpu.VMEM((4, PAIR_DEV, 128), f32) for unit in range(UNITS)),
         ],
         compiler_params=pltpu.CompilerParams(
             collective_id=0, has_side_effects=True, vmem_limit_bytes=60 * 2**20

time: 73.7 us -> 72.6 us (0.985)
  Pallas kernels: 72.9 us -> 71.8 us
    pallas_call x1, Pallas kernels: 70.8 us -> 69.7 us  [shards(): pl.pallas_call(kernel, out_shape=(band, band, band, jax.ShapeDtypeStruct(...]
where the time goes in v7:
time: 72.6 us; the launch traced here: 72.5 us
  Pallas kernels  71.8 us (99%)
    pallas_call x1, Pallas kernels, shards(): pl.pallas_call(kernel, out_shape=(band, band, band, jax.ShapeDtypeStruct(...  69.7 us
    pallas_call x1, Pallas kernels, shards(): pl.pallas_call(store, out_shape=(band, band, band, jax.ShapeDtypeStruct((...  2.15 us

profile of v7, /device:TPU:1, one launch (start us, length us, event | category | flops | bytes accessed | tf_op | source)
XLA Modules:
  0.0 72.5 jit_solution(2905022823445238383)
XLA Ops:
  0.6 69.7 %align.1 = (f32[768,128]{1,0:T(8,128)}, f32[768,128]{1,0:T(8,128)}, f32[768,128]{1,0:T(8,128)}, f32[1,8]{1,0:T(1,128)}) custom-call(f32[768,128]{1,0:T(8,128)} %bitcast.40, f32[768,128]{1,0:T(8,128)} %bitcast.41, f32[768,128]{1,0:T(8,128)} %bitcast.42, bf16[6,8,24576]{2,1,0:T(8,128)(2,1)} %bitcast.38, bf16[3072,128]{1,0:T(8,128)(2,1)} %bitcast.39, ...), custom_call_target="tpu_custom_call" | custom-call | tf_op jit(solution)/shard_map/align/pallas_call | solution.py:823
  70.3 2.2 %store.1 = (f32[768,128]{1,0:T(8,128)}, f32[768,128]{1,0:T(8,128)}, f32[768,128]{1,0:T(8,128)}, f32[1,8]{1,0:T(1,128)}) custom-call(f32[768,128]{1,0:T(8,128)} %get-tuple-element.12.log_in, f32[768,128]{1,0:T(8,128)} %get-tuple-element.13.one_in, f32[768,128]{1,0:T(8,128)} %get-tuple-element.14.two_in, f32[1,8]{1,0:T(1,128)} %get-tuple-element.15.scale_in), custom_call_target="tpu_custom_call" | custom-call | tf_op jit(solution)/shard_map/store/pallas_call | solution.py:893

commit v8 on v7

--- a/solution.py
+++ b/solution.py
@@ -29,9 +29,9 @@
 UNIT_ROWS = BAND_ROWS // UNITS
 OWN_STEPS = 4
 STEPS = (2, 1, 3)
-TILE = 12
+TILE = 24
 PART = 4
-ADAM = 6
+ADAM = 8
 UNROLL = 8
 LEVELS = 32700.0
 
@@ -174,15 +174,9 @@
     offsets = [(a, b, c) for a in range(XS) for b in range(YS) for c in range(ZS) if (a, b, c) != (0, 0, 0)]
     offsets.sort(key=lambda o: -sum(min(d, 4 - d) for d in o))
 
-    def greet_chip(k, carry):
-        x = (my_x + k // OWNERS) % XS
-        y = (my_y + k // ZS) % YS
-        z = (my_z + k) % ZS
-        pl.semaphore_signal(barrier, 1, device_id=(x * 2 + my_core, y * ZS + z), device_id_type=MESH)
-        return carry
-
     pl.semaphore_signal(barrier, 1, device_id=(my_img + 1 - 2 * my_core, my_pair), device_id_type=MESH)
-    lax.fori_loop(1, CHIPS, greet_chip, 0)
+    for a, b, c in offsets:
+        pl.semaphore_signal(barrier, 1, device_id=(xs[a] * 2 + my_core, ys[b] * ZS + zs[c]), device_id_type=MESH)
 
     sub = lax.broadcasted_iota(jnp.int32, (8, 128), 0)
     lane = lax.broadcasted_iota(jnp.int32, (8, 128), 1)

time: 72.6 us -> 71.2 us (0.981)
  Pallas kernels: 71.8 us -> 70.4 us
    pallas_call x1, Pallas kernels: 69.7 us -> 68.2 us  [shards(): pl.pallas_call(kernel, out_shape=(band, band, band, jax.ShapeDtypeStruct(...]
where the time goes in v8:
time: 71.2 us; the launch traced here: 71 us
  Pallas kernels  70.4 us (99%)
    pallas_call x1, Pallas kernels, shards(): pl.pallas_call(kernel, out_shape=(band, band, band, jax.ShapeDtypeStruct(...  68.2 us
    pallas_call x1, Pallas kernels, shards(): pl.pallas_call(store, out_shape=(band, band, band, jax.ShapeDtypeStruct((...  2.15 us

profile of v8, /device:TPU:1, one launch (start us, length us, event | category | flops | bytes accessed | tf_op | source)
XLA Modules:
  0.0 71.0 jit_solution(6572659397685263246)
XLA Ops:
  0.6 68.2 %align.1 = (f32[768,128]{1,0:T(8,128)}, f32[768,128]{1,0:T(8,128)}, f32[768,128]{1,0:T(8,128)}, f32[1,8]{1,0:T(1,128)}) custom-call(f32[768,128]{1,0:T(8,128)} %bitcast.40, f32[768,128]{1,0:T(8,128)} %bitcast.41, f32[768,128]{1,0:T(8,128)} %bitcast.42, bf16[6,8,24576]{2,1,0:T(8,128)(2,1)} %bitcast.38, bf16[3072,128]{1,0:T(8,128)(2,1)} %bitcast.39, ...), custom_call_target="tpu_custom_call" | custom-call | tf_op jit(solution)/shard_map/align/pallas_call | solution.py:817
  68.9 2.2 %store.1 = (f32[768,128]{1,0:T(8,128)}, f32[768,128]{1,0:T(8,128)}, f32[768,128]{1,0:T(8,128)}, f32[1,8]{1,0:T(1,128)}) custom-call(f32[768,128]{1,0:T(8,128)} %get-tuple-element.12.log_in, f32[768,128]{1,0:T(8,128)} %get-tuple-element.13.one_in, f32[768,128]{1,0:T(8,128)} %get-tuple-element.14.two_in, f32[1,8]{1,0:T(1,128)} %get-tuple-element.15.scale_in), custom_call_target="tpu_custom_call" | custom-call | tf_op jit(solution)/shard_map/store/pallas_call | solution.py:887
